TPU v7x, 256 devices: a whole 4x4x8 slice. The times are simulated.
256 devices in a mesh: blk: 8 (over y, x_lo), group: 32 (over x_hi, z, core).
Axes of the slice: x: 4 (x_hi: 2, x_lo: 2; x = x_hi * 2 + x_lo), y: 4, z: 8, core: 2. Of those that a mesh axis runs over, the one named last changes fastest.
Arguments:
- patches: bfloat16 [65536, 1152], P(('blk', 'group')), may hold values from -400 to 400
- row_owner: int32 [8, 32, 256], P('blk'), may hold values from 0 to 31, as said below
- row_slot: int32 [8, 32, 256], P('blk'), may hold values from 0 to 3, as said below
- text_embed: bfloat16 [1024, 1152], P(('blk', 'group')), may hold values from -6 to 6
- probe_query: float32 [1152], replicated, may hold values from -5 to 5
- w_key: bfloat16 [1152, 1152], replicated, may hold values from -0.1875 to 0.1875
- w_value: bfloat16 [1152, 1152], replicated, may hold values from -0.1875 to 0.1875
- w_out: bfloat16 [1152, 1152], replicated, may hold values from -0.1875 to 0.1875
- logit_scale: float32 [1], replicated, may hold values from 1.6 to 2.3
- logit_bias: float32 [1], replicated, may hold values from -1.5 to -0.5
Outputs:
- grad_patches: bfloat16 [65536, 1152], P(('blk', 'group'))
- grad_text: bfloat16 [1024, 1152], P(('blk', 'group'))
Inputs may be any that keep to these rules, and one draw needn't show every extreme that they name: `row_owner`: in each blk index, the rows of one device name one owner at most 24 times; in every draw some owner of each blk index is named exactly 24 times by every device of that blk index. `row_slot`: every slot of every owner receives at least one row of its blk index.
All inputs are finite; a program needn't handle non-finite values.
Results may differ from a plain program's by a relative error of at most 0.002.
Values may be sent and summed in bfloat16 or wider, within the bound.
A program may use at most 128 MiB of HBM per device.

v0:
```python
import math

import jax
import jax.numpy as jnp
from jax import lax
from jax.sharding import PartitionSpec as P

HEADS = 16


loss_scale = 256.0
norm_eps = 1e-06
highest = lax.Precision.HIGHEST


def passed_along(block, axis, distance):
    devices = range(lax.axis_size(axis))
    route = [((i - distance) % len(devices), i) for i in devices]
    return lax.ppermute(block, axis, route)


def unit_rows(matrix):
    length = jnp.sqrt(jnp.sum(matrix * matrix, axis=-1, keepdims=True) + norm_eps)
    return (matrix / length, length)


def attend(scores, member):
    masked = jnp.where(member[:, None, :], scores[None, :, :], -jnp.inf)
    peak = jnp.max(masked, axis=2, keepdims=True)
    raised = jnp.exp(masked - peak)
    return raised / jnp.sum(raised, axis=2, keepdims=True)


def local(
    patches,
    row_owner,
    row_slot,
    text_embed,
    probe_query,
    w_key,
    w_value,
    w_out,
    logit_scale,
    logit_bias,
):
    groups = lax.axis_size("group")
    rounds = lax.axis_size("blk")
    source_rows, width = patches.shape
    images = text_embed.shape[0]
    head_count = HEADS
    head_width = width // head_count
    capacity = 3 * source_rows // groups
    slots_all = groups * capacity
    here = lax.axis_index("group")
    cycle_pos = lax.axis_index("blk")
    owners = row_owner[0]
    slots = row_slot[0]
    query_scaled = probe_query / math.sqrt(head_width)
    query_heads = query_scaled.reshape(head_count, head_width)
    query_table = (
        jnp.eye(head_count, dtype=jnp.float32)[:, :, None] * query_heads[None, :, :]
    ).reshape(head_count, width)
    image_range = jnp.arange(images, dtype=jnp.int32)
    span = groups * images
    own_owner = lax.dynamic_index_in_dim(owners, here, 0, keepdims=False)
    hits = own_owner[None, :] == jnp.arange(groups, dtype=jnp.int32)[:, None]
    send_rank = jnp.sum((jnp.cumsum(hits.astype(jnp.int32), axis=1) - 1) * hits, axis=0)
    position = own_owner * capacity + send_rank
    outgoing = (
        jnp.zeros((slots_all, width), jnp.bfloat16)
        .at[position]
        .set(patches)
        .reshape(groups, capacity, width)
    )
    mine = owners == here
    arrival_rank = jnp.cumsum(mine.astype(jnp.int32), axis=1) - 1
    source_ids = jnp.broadcast_to(jnp.arange(groups, dtype=jnp.int32)[:, None], owners.shape)
    target = jnp.where(mine, arrival_rank, capacity)
    slot_table = (
        jnp.full((groups, capacity), -1, jnp.int32).at[source_ids, target].set(slots, mode="drop")
    )
    member = slot_table.reshape(slots_all)[None, :] == image_range[:, None]
    rows = lax.all_to_all(outgoing, "group", split_axis=0, concat_axis=0, tiled=True)
    keys = jnp.einsum("sce,ef->scf", rows, w_key, preferred_element_type=jnp.float32)
    values = jnp.einsum("sce,ef->scf", rows, w_value, preferred_element_type=jnp.float32)
    keys = keys.reshape(slots_all, width)
    values3 = values.reshape(slots_all, head_count, head_width)
    scores = jnp.dot(query_table, keys.T, precision=highest)
    weights = attend(scores, member)
    pooled3 = jnp.einsum("ihr,rhd->ihd", weights, values3, precision=highest)
    pooled = pooled3.reshape(images, width)
    embeds = jnp.dot(pooled, w_out, precision=highest, preferred_element_type=jnp.float32)
    image_unit, image_norm = unit_rows(embeds)
    temper = jnp.exp(logit_scale[0])
    bias_value = logit_bias[0]
    own_unit, own_norm = unit_rows(text_embed.astype(jnp.float32))
    group_texts = lax.all_gather(text_embed, "group", axis=0, tiled=True)
    positive = (
        jnp.arange(span, dtype=jnp.int32)[None, :] == here * images + image_range[:, None]
    ).astype(jnp.float32)
    image_dunit = jnp.zeros((images, width), jnp.float32)
    store = jnp.zeros((rounds, span, width), jnp.float32)
    current = group_texts
    for rotation in range(rounds):
        if rotation > 0:
            current = passed_along(current, "blk", 1)
        absorb_image_dunit = image_dunit
        absorb_store = store
        block_unit = unit_rows(current.astype(jnp.float32))[0]
        logits = temper * jnp.dot(image_unit, block_unit.T, precision=highest) + bias_value
        signal = jax.nn.sigmoid(logits)
        if rotation == 0:
            signal = signal - positive
        grads = loss_scale * signal
        absorb_image_dunit = absorb_image_dunit + temper * jnp.dot(
            grads, block_unit, precision=highest
        )
        anchor = (cycle_pos - rotation) % rounds
        whole = temper * jnp.dot(grads.T, image_unit, precision=highest)
        absorb_store = lax.dynamic_update_index_in_dim(absorb_store, whole, anchor, 0)
        image_dunit = absorb_image_dunit
        store = absorb_store
    text_dunit = lax.psum_scatter(
        store.reshape(rounds * span, width), ("blk", "group"), scatter_dimension=0, tiled=True
    )
    grad_text = (
        (text_dunit - own_unit * jnp.sum(own_unit * text_dunit, axis=1, keepdims=True)) / own_norm
    ).astype(jnp.bfloat16)
    embed_grad = (
        image_dunit - image_unit * jnp.sum(image_unit * image_dunit, axis=1, keepdims=True)
    ) / image_norm
    pooled_grad = jnp.dot(
        embed_grad, w_out.T, precision=highest, preferred_element_type=jnp.float32
    )
    pooled_grad3 = pooled_grad.reshape(images, head_count, head_width)
    dweights = jnp.einsum("ihd,rhd->ihr", pooled_grad3, values3, precision=highest)
    dscores = weights * (dweights - jnp.sum(weights * dweights, axis=2, keepdims=True))
    key_grad = jnp.einsum("ihr,hd->rhd", dscores, query_heads, precision=highest).reshape(
        slots_all, width
    )
    value_grad = jnp.einsum("ihr,ihd->rhd", weights, pooled_grad3, precision=highest).reshape(
        slots_all, width
    )
    row_grad = jnp.dot(key_grad, w_key.T, precision=highest, preferred_element_type=jnp.float32)
    row_grad = row_grad + jnp.dot(
        value_grad, w_value.T, precision=highest, preferred_element_type=jnp.float32
    )
    returned = lax.all_to_all(
        row_grad.astype(jnp.bfloat16).reshape(groups, capacity, width),
        "group",
        split_axis=0,
        concat_axis=0,
        tiled=True,
    )
    grad_patches = returned.reshape(slots_all, width)[position]
    return (grad_patches, grad_text)


def solution(mesh):
    placed = (
        P(("blk", "group"), None),
        P("blk", None, None),
        P("blk", None, None),
        P(("blk", "group"), None),
        P(),
        P(),
        P(),
        P(),
        P(),
        P(),
    )
    return jax.shard_map(
        local,
        mesh=mesh,
        in_specs=placed,
        out_specs=(P(("blk", "group"), None), P(("blk", "group"), None)),
        check_vma=False,
    )
```

profile of v0, /device:TPU:1, one launch (start us, length us, event | category | flops | bytes accessed | tf_op | source)
XLA Modules:
  0.0 586.4 jit_solution(1578485263148073161)
XLA Ops:
  9.7 3.6 scatter_custom_fusion
  13.3 12.6 %all-to-all-start = ((bf16[32,24,1152]{2,1,0:T(8,128)(2,1)}), bf16[32,24,1152]{2,1,0:T(8,128)(2,1)}, u32[]{:S(2)}, u32[]{:S(2)}) async-start(bf16[32,24,1152]{2,1,0:T(8,128)(2,1)} %bitcast.108), calls=%async_computation | async-start | bytes 3538944 | tf_op jit(solution)/shard_map/all_to_all | solution.py:83
  26.0 75.5 %all-gather = bf16[32,4,1152]{2,1,0:T(4,128)(2,1)S(1)} all-gather(bf16[1,4,1152]{2,1,0:T(4,128)(2,1)S(1)} %bitcast.113), channel_id=1, replica_groups=mesh['blk'=8,'group'=32] {'group'}, dimensions={0}, use_global_device_ids=true | all-gather | bytes 304128 | tf_op jit(solution)/shard_map/all_gather | solution.py:97
  103.7 30.4 %scatter_custom_fusion.1 = s32[768]{0:T(1024)S(1)} fusion(s32[8192]{0:T(1024)S(1)} %bitcast.116, s32[8192]{0:T(1024)S(1)} %bitcast.117, s32[]{:T(128)} %constant.110.clone.1), kind=kCustom, calls=%fused_computation.192 | custom fusion | bytes 3076
  135.9 2.2 collective-permute-start.1
  138.3 7.9 %collective-permute-done.1 = bf16[128,1152]{1,0:T(8,128)(2,1)S(1)} collective-permute-done((bf16[128,1152]{1,0:T(8,128)(2,1)S(1)}, bf16[128,1152]{1,0:T(8,128)(2,1)S(1)}, u32[]{:S(2)}, u32[]{:S(2)}) %collective-permute-start.1) | collective-permute-done | bytes 294944 | tf_op jit(solution)/shard_map/ppermute | solution.py:19
  147.1 8.5 %collective-permute-done.2 = bf16[128,1152]{1,0:T(8,128)(2,1)S(1)} collective-permute-done((bf16[128,1152]{1,0:T(8,128)(2,1)S(1)}, bf16[128,1152]{1,0:T(8,128)(2,1)S(1)}, u32[]{:S(2)}, u32[]{:S(2)}) %collective-permute-start.2) | collective-permute-done | bytes 294944 | tf_op jit(solution)/shard_map/ppermute | solution.py:19
  156.4 7.5 %collective-permute-done.3 = bf16[128,1152]{1,0:T(8,128)(2,1)S(1)} collective-permute-done((bf16[128,1152]{1,0:T(8,128)(2,1)S(1)}, bf16[128,1152]{1,0:T(8,128)(2,1)S(1)}, u32[]{:S(2)}, u32[]{:S(2)}) %collective-permute-start.3) | collective-permute-done | bytes 294944 | tf_op jit(solution)/shard_map/ppermute | solution.py:19
  164.8 6.8 %collective-permute-done.4 = bf16[128,1152]{1,0:T(8,128)(2,1)S(1)} collective-permute-done((bf16[128,1152]{1,0:T(8,128)(2,1)S(1)}, bf16[128,1152]{1,0:T(8,128)(2,1)S(1)}, u32[]{:S(2)}, u32[]{:S(2)}) %collective-permute-start.4) | collective-permute-done | bytes 294944 | tf_op jit(solution)/shard_map/ppermute | solution.py:19
  172.5 6.8 %collective-permute-done.5 = bf16[128,1152]{1,0:T(8,128)(2,1)S(1)} collective-permute-done((bf16[128,1152]{1,0:T(8,128)(2,1)S(1)}, bf16[128,1152]{1,0:T(8,128)(2,1)S(1)}, u32[]{:S(2)}, u32[]{:S(2)}) %collective-permute-start.5) | collective-permute-done | bytes 294944 | tf_op jit(solution)/shard_map/ppermute | solution.py:19
  180.2 7.3 %collective-permute-done.6 = bf16[128,1152]{1,0:T(8,128)(2,1)S(1)} collective-permute-done((bf16[128,1152]{1,0:T(8,128)(2,1)S(1)}, bf16[128,1152]{1,0:T(8,128)(2,1)S(1)}, u32[]{:S(2)}, u32[]{:S(2)}) %collective-permute-start.6) | collective-permute-done | bytes 294944 | tf_op jit(solution)/shard_map/ppermute | solution.py:19
  188.4 6.8 %fusion.2 = f32[32,24,1152]{2,1,0:T(8,128)} fusion(bf16[32,24,1152]{2,1,0:T(8,128)(2,1)} %all-to-all-done, bf16[1152,1152]{1,0:T(8,128)(2,1)} %param.16), kind=kOutput, calls=%fused_computation.6 | convolution fusion | flops 2038431744 | bytes 7962624 | tf_op jit(solution)/shard_map/sce,ef->scf/dot_general | solution.py:85
  195.2 8.0 %reshape.313 = f32[768,16,72]{2,1,0:T(8,128)} reshape(f32[32,24,1152]{2,1,0:T(8,128)} %fusion.2) | data formatting | bytes 7077888 | tf_op jit(solution)/shard_map/reshape | solution.py:87
  203.2 5.9 %copy.37 = f32[768,16,72]{0,2,1:T(8,128)} copy(f32[768,16,72]{2,1,0:T(8,128)} %reshape.313) | data formatting | bytes 7077888 | tf_op jit(solution)/shard_map/reshape | solution.py:87
  209.2 4.2 fusion.4
  213.4 3.0 fusion.128
  216.7 3.1 convolution_bitcast_fusion.1
  220.0 3.0 multiply_reduce_fusion.4
  233.3 2.2 fusion.112
  235.6 4.0 convolution_bitcast_fusion
  239.6 3.1 fusion.105
  243.7 14.1 %fusion.129 = f32[768,1152]{1,0:T(8,128)S(1)} fusion(f32[768,1152]{0,1:T(8,128)S(1)} %bitcast.110, bf16[1152,1152]{1,0:T(8,128)(2,1)S(1)} %copy-done), kind=kOutput, calls=%fused_computation.213 | convolution fusion | flops 12230590464 | bytes 9732096 | tf_op jit(solution)/shard_map/dot_general | solution.py:144
  257.9 15.7 %fusion.1 = bf16[768,1152]{1,0:T(8,128)(2,1)} fusion(f32[768,1152]{1,0:T(8,128)S(1)} %fusion.129, f32[768,1152]{0,1:T(8,128)S(1)} %bitcast.111, bf16[1152,1152]{1,0:T(8,128)(2,1)S(1)} %copy-done.23), kind=kOutput, calls=%fused_computation.5 | convolution fusion | flops 12232359936 | bytes 11501568 | tf_op jit(solution)/shard_map/dot_general | solution.py:145
  273.5 10.9 %all-to-all-start.1 = ((bf16[32,24,1152]{2,1,0:T(8,128)(2,1)}), bf16[32,24,1152]{2,1,0:T(8,128)(2,1)}, u32[]{:S(2)}, u32[]{:S(2)}) async-start(bf16[32,24,1152]{2,1,0:T(8,128)(2,1)} %bitcast.112), calls=%async_computation.1 | async-start | bytes 3538944 | tf_op jit(solution)/shard_map/all_to_all | solution.py:148
  284.6 2.5 broadcast_in_dim.101
  287.2 1.6 fusion.7
  288.8 1.6 fusion.9
  290.4 1.6 fusion.11
  295.1 1.6 fusion.17
  298.3 1.6 fusion.21
  300.0 272.7 %all-reduce.3.cloned.1.call-done = f32[1024,1152]{1,0:T(8,128)} async-done(((f32[1024,1152]{1,0:T(8,128)}), f32[1024,1152]{1,0:T(8,128)}) %all-reduce.3.cloned.1.call-update) | async-done | bytes 4718608
  575.2 4.2 gather_fusion
  (143 shorter events, 29.4 us)
Async XLA Ops:
  7.2 202.0 %copy-start = (bf16[1152,1152]{1,0:T(8,128)(2,1)S(1)}, bf16[1152,1152]{1,0:T(8,128)(2,1)}, u32[]{:S(2)}) copy-start(bf16[1152,1152]{1,0:T(8,128)(2,1)} %param.15) | copy-start | bytes 7962628
  7.2 94.8 %copy-start.16 = (s32[1,32,256]{2,1,0:T(8,128)S(1)}, s32[1,32,256]{2,1,0:T(8,128)}, u32[]{:S(2)}) copy-start(s32[1,32,256]{2,1,0:T(8,128)} %param.11) | copy-start | bytes 98308
  7.2 18.8 %copy-start.15 = (bf16[4,1152]{1,0:T(4,128)(2,1)S(1)}, bf16[4,1152]{1,0:T(4,128)(2,1)}, u32[]{:S(2)}) copy-start(bf16[4,1152]{1,0:T(4,128)(2,1)} %param.13) | copy-start | bytes 27652
  7.2 94.8 %copy-start.18 = (f32[1152]{0:T(1024)S(1)}, f32[1152]{0:T(1024)}, u32[]{:S(2)}) copy-start(f32[1152]{0:T(1024)} %param.14) | copy-start | bytes 13828
  8.9 94.4 %copy-start.22 = (s32[2]{0:T(128)S(1)}, s32[2]{0:T(128)}, u32[]{:S(2)}) copy-start(s32[2]{0:T(128)} %constant.139) | copy-start | bytes 28
  9.7 92.2 %copy-start.19 = (s32[256,1]{0,1:T(1,128)}, s32[256,1]{0,1:T(1,128)S(1)}, u32[]{:S(2)}) copy-start(s32[256,1]{0,1:T(1,128)S(1)} %compare_select_fusion.1) | copy-start | bytes 3076
  9.7 93.6 %copy-start.21 = (s32[2]{0:T(128)S(1)}, s32[2]{0:T(128)}, u32[]{:S(2)}) copy-start(s32[2]{0:T(128)} %constant.136) | copy-start | bytes 28
  9.7 93.9 %copy-start.17 = (s32[1,32,256]{2,1,0:T(8,128)S(1)}, s32[1,32,256]{2,1,0:T(8,128)}, u32[]{:S(2)}) copy-start(s32[1,32,256]{2,1,0:T(8,128)} %param.12) | copy-start | bytes 98308
  13.3 175.0 %all-to-all-start = ((bf16[32,24,1152]{2,1,0:T(8,128)(2,1)}), bf16[32,24,1152]{2,1,0:T(8,128)(2,1)}, u32[]{:S(2)}, u32[]{:S(2)}) async-start(bf16[32,24,1152]{2,1,0:T(8,128)(2,1)} %bitcast.108), calls=%async_computation | async-start | bytes 3538944 | tf_op jit(solution)/shard_map/all_to_all | solution.py:83
  101.5 34.4 %collective-permute-start = (bf16[128,1152]{1,0:T(8,128)(2,1)S(1)}, bf16[128,1152]{1,0:T(8,128)(2,1)S(1)}, u32[]{:S(2)}, u32[]{:S(2)}) collective-permute-start(bf16[128,1152]{1,0:T(8,128)(2,1)S(1)} %reshape.350), channel_id=1, source_target_pairs={{224,0},{0,32},{32,64},{64,96},{96,128},{128,160},{160,192},{192,2... | collective-permute-start | bytes 884744 | tf_op jit(solution)/shard_map/ppermute | solution.py:19
  135.9 10.3 %collective-permute-start.1 = (bf16[128,1152]{1,0:T(8,128)(2,1)S(1)}, bf16[128,1152]{1,0:T(8,128)(2,1)S(1)}, u32[]{:S(2)}, u32[]{:S(2)}) collective-permute-start(bf16[128,1152]{1,0:T(8,128)(2,1)S(1)} %collective-permute-done), channel_id=1, source_target_pairs={{224,0},{0,32},{32,64},{64,96},{96,128},{128,160},{160,192},{192,2... | collective-permute-start | bytes 884744 | tf_op jit(solution)/shard_map/ppermute | solution.py:19
  146.3 0.7 copy-start.3
  146.3 9.3 %collective-permute-start.2 = (bf16[128,1152]{1,0:T(8,128)(2,1)S(1)}, bf16[128,1152]{1,0:T(8,128)(2,1)S(1)}, u32[]{:S(2)}, u32[]{:S(2)}) collective-permute-start(bf16[128,1152]{1,0:T(8,128)(2,1)S(1)} %collective-permute-done.1), channel_id=1, source_target_pairs={{224,0},{0,32},{32,64},{64,96},{96,128},{128,160},{160,192},{192,2... | collective-permute-start | bytes 884744 | tf_op jit(solution)/shard_map/ppermute | solution.py:19
  155.6 8.4 %collective-permute-start.3 = (bf16[128,1152]{1,0:T(8,128)(2,1)S(1)}, bf16[128,1152]{1,0:T(8,128)(2,1)S(1)}, u32[]{:S(2)}, u32[]{:S(2)}) collective-permute-start(bf16[128,1152]{1,0:T(8,128)(2,1)S(1)} %collective-permute-done.2), channel_id=1, source_target_pairs={{224,0},{0,32},{32,64},{64,96},{96,128},{128,160},{160,192},{192,2... | collective-permute-start | bytes 884744 | tf_op jit(solution)/shard_map/ppermute | solution.py:19
  164.0 0.7 copy-start.7
  164.0 7.7 %collective-permute-start.4 = (bf16[128,1152]{1,0:T(8,128)(2,1)S(1)}, bf16[128,1152]{1,0:T(8,128)(2,1)S(1)}, u32[]{:S(2)}, u32[]{:S(2)}) collective-permute-start(bf16[128,1152]{1,0:T(8,128)(2,1)S(1)} %collective-permute-done.3), channel_id=1, source_target_pairs={{224,0},{0,32},{32,64},{64,96},{96,128},{128,160},{160,192},{192,2... | collective-permute-start | bytes 884744 | tf_op jit(solution)/shard_map/ppermute | solution.py:19
  171.7 7.7 %collective-permute-start.5 = (bf16[128,1152]{1,0:T(8,128)(2,1)S(1)}, bf16[128,1152]{1,0:T(8,128)(2,1)S(1)}, u32[]{:S(2)}, u32[]{:S(2)}) collective-permute-start(bf16[128,1152]{1,0:T(8,128)(2,1)S(1)} %collective-permute-done.4), channel_id=1, source_target_pairs={{224,0},{0,32},{32,64},{64,96},{96,128},{128,160},{160,192},{192,2... | collective-permute-start | bytes 884744 | tf_op jit(solution)/shard_map/ppermute | solution.py:19
  179.4 0.7 copy-start.11
  179.4 8.1 %collective-permute-start.6 = (bf16[128,1152]{1,0:T(8,128)(2,1)S(1)}, bf16[128,1152]{1,0:T(8,128)(2,1)S(1)}, u32[]{:S(2)}, u32[]{:S(2)}) collective-permute-start(bf16[128,1152]{1,0:T(8,128)(2,1)S(1)} %collective-permute-done.5), channel_id=1, source_target_pairs={{224,0},{0,32},{32,64},{64,96},{96,128},{128,160},{160,192},{192,2... | collective-permute-start | bytes 884744 | tf_op jit(solution)/shard_map/ppermute | solution.py:19
  187.5 0.7 copy-start.13
  213.4 3.3 copy-start.1
  223.7 1.8 copy-start.4
  225.0 1.8 copy-start.6
  226.2 1.8 copy-start.8
  227.5 2.0 copy-start.10
  228.7 2.0 copy-start.12
  230.1 1.8 copy-start.14
  231.4 1.9 copy-start.2
  243.7 14.1 %copy-start.23 = (bf16[1152,1152]{1,0:T(8,128)(2,1)S(1)}, bf16[1152,1152]{1,0:T(8,128)(2,1)}, u32[]{:S(2)}) copy-start(bf16[1152,1152]{1,0:T(8,128)(2,1)} %param.16) | copy-start | bytes 7962628
  273.5 301.6 %all-to-all-start.1 = ((bf16[32,24,1152]{2,1,0:T(8,128)(2,1)}), bf16[32,24,1152]{2,1,0:T(8,128)(2,1)}, u32[]{:S(2)}, u32[]{:S(2)}) async-start(bf16[32,24,1152]{2,1,0:T(8,128)(2,1)} %bitcast.112), calls=%async_computation.1 | async-start | bytes 3538944 | tf_op jit(solution)/shard_map/all_to_all | solution.py:148
  284.4 288.3 %all-reduce.3.cloned.1.call-start = ((), (), s32[]{:S(2)}) async-start(), calls=%async_computation.2 | async-start | bytes 9437184
  293.6 6.3 %copy-start.20 = (s32[256,1]{0,1:T(1,128)S(1)}, s32[256,1]{0,1:T(1,128)}, u32[]{:S(2)}) copy-start(s32[256,1]{0,1:T(1,128)} %copy-done.19) | copy-start | bytes 3076
  (2 other events, 1.4 us)
Sparse Core Ops, SparseCore 0:
  300.0 272.7 all-reduce.2
where the time goes:
time: 596 us; the launch traced here: 586 us
  waiting for transfers between devices  318 us (53%)
  matrix products  81.9 us (14%)
  blocking collectives  75.5 us (13%)
  local copies, waits for them, and re-layouts  60.7 us (10%)
  starting transfers between devices  26.9 us (5%)
  between operations  16.3 us (3%)
  other arithmetic  7.58 us (1%)
    unnamed x2, waiting for transfers between devices  273 us
    all_gather x1, blocking collectives, local(): group_texts = lax.all_gather(text_embed, 'group', axis=0, tiled=True)  75.5 us
    ppermute x7, waiting for transfers between devices, passed_along(): return lax.ppermute(block, axis, route)  44.8 us
    unnamed x53, local copies, waits for them, and re-layouts  34.5 us
    dot_general x1, matrix products, local(): jnp.dot(value_grad, w_value.T, precision=highest, preferred_element_type=...  15.7 us
    dot_general x1, matrix products, local(): jnp.dot(key_grad, w_key.T, precision=highest, preferred_element_type=jnp....  14.1 us
    reshape x2, local copies, waits for them, and re-layouts, local(): values3 = values.reshape(slots_all, head_count, head_width)  13.9 us
    dot_general x8, matrix products, local(): whole = temper * jnp.dot(grads.T, image_unit, precision=highest)  12.6 us
  transfers between devices with their start and end apart: 10, of which 7 were waited for; matrix products, arithmetic and copies ran while one was open for 9% of the time, Pallas kernels for 0%

commit v1 on v0

v1 whole, which is shorter than its diff:
```python
import functools
import math

import jax
import jax.numpy as jnp
from jax import lax
from jax.experimental import pallas as pl
from jax.experimental.pallas import tpu as pltpu
from jax.sharding import PartitionSpec as P

HEADS = 16
IMG = 4
LANES = 128
CHUNK = 384
LOSS_SCALE = 256.0
EPS = 1e-06
LOW = -1e30

F32 = jnp.float32
BF16 = jnp.bfloat16
MESH = pl.DeviceIdType.MESH


def mm(a, b):
    return lax.dot_general(a, b, (((1,), (0,)), ((), ())), preferred_element_type=F32)


def mm_nt(a, b):
    return lax.dot_general(a, b, (((1,), (1,)), ((), ())), preferred_element_type=F32)


def pieces(x, count):
    out = []
    for _ in range(count - 1):
        top = x.astype(BF16).astype(F32)
        out.append(top)
        x = x - top
    out.append(x.astype(BF16).astype(F32))
    return out


def stacked(x, count):
    return jnp.concatenate(pieces(x, count), axis=0).astype(BF16)


def small_rows(x, buf):
    for k, piece in enumerate(pieces(x, 3)):
        buf[k * IMG : (k + 1) * IMG, :] = piece
    return buf[...].astype(BF16)


def three(y):
    return y[0:IMG] + y[IMG : 2 * IMG] + y[2 * IMG : 3 * IMG]


def kernel(
    nb,
    ng,
    nz,
    patches,
    owner,
    slot,
    text,
    probe,
    w_key,
    w_value,
    w_out,
    logit_scale,
    logit_bias,
    g_patch,
    g_text,
    wk,
    wv,
    wo,
    p,
    v,
    st,
    hm,
    kp3,
    kpr,
    ot,
    et,
    acc_out,
    acc_in,
    fs,
    rows16,
    pooled_buf,
    unit_all,
    u32,
    di_out,
    di_in,
    t_all,
    tf,
    t_out,
    t_in,
    pg_all,
    pgm,
    ob,
    vg,
    load_sem,
    pair_send,
    pair_recv,
    text_send,
    text_recv,
    acc_send,
    acc_recv,
    unit_send,
    unit_recv,
    di_send,
    di_recv,
    td_send,
    td_recv,
    pg_send,
    pg_recv,
):
    nq = ng // 2
    nxh = nq // nz
    nplane = nb * nxh * 2
    mine = nq * IMG
    rows, width = patches.shape
    chunks = width // CHUNK
    head_width = width // HEADS
    blk = lax.axis_index("blk")
    grp = lax.axis_index("group")
    core = grp % 2
    q = grp // 2
    z = q % nz
    xh = q // nz
    sib = q * 2 + (1 - core)
    place = (blk * nxh + xh) * 2 + core

    def group_peer(d):
        k = (q + d) % nq
        return k, (blk, k * 2 + core)

    def line_peer(d):
        k = (z + d) % nz
        return k, (blk, (xh * nz + k) * 2 + core)

    def plane_peer(d):
        k = (place + d) % nplane
        return k, (k // (2 * nxh), (((k // 2) % nxh) * nz + z) * 2 + k % 2)

    def remote(src, dst, send, recv, device):
        return pltpu.make_async_remote_copy(
            src_ref=src,
            dst_ref=dst,
            send_sem=send,
            recv_sem=recv,
            device_id=device,
            device_id_type=MESH,
        )

    def each(count, act):
        def step(d, carry):
            act(d)
            return carry

        lax.fori_loop(1, count, step, 0)

    def spread(peer, count, src_of, dst, me, send, recv):
        def act(d):
            k, device = peer(d)
            remote(src_of(k), dst.at[me], send.at[k], recv.at[me], device).start()

        each(count, act)

    def gather_wait(peer, count, dst, send, recv):
        def act(d):
            k, device = peer(d)
            remote(dst.at[k], dst.at[k], send.at[k], recv.at[k], device).wait_recv()

        each(count, act)

    def send_wait(peer, count, src_of, send, recv):
        def act(d):
            k, device = peer(d)
            remote(src_of(k), src_of(k), send.at[k], recv.at[k], device).wait_send()

        each(count, act)

    load_k = pltpu.make_async_copy(w_key, wk, load_sem.at[0])
    load_p = pltpu.make_async_copy(patches, p.at[0], load_sem.at[1])
    load_v = pltpu.make_async_copy(w_value, wv, load_sem.at[2])
    load_o = pltpu.make_async_copy(w_out, wo, load_sem.at[3])
    load_k.start()
    load_p.start()
    load_v.start()
    load_o.start()

    barrier = pltpu.get_barrier_semaphore()

    def greet(peer):
        def act(d):
            pl.semaphore_signal(barrier, inc=1, device_id=peer(d)[1], device_id_type=MESH)

        return act

    each(nplane, greet(plane_peer))
    each(nq, greet(group_peer))

    row_i = lax.broadcasted_iota(jnp.int32, (LANES, width), 0)
    col_i = lax.broadcasted_iota(jnp.int32, (LANES, width), 1)
    first = (row_i & (HEADS - 1)) * head_width
    in_head = (col_i >= first) & (col_i < first + head_width)
    hm[...] = jnp.where(in_head & (row_i < 3 * HEADS), 1.0, 0.0).astype(BF16)
    q3 = pieces(probe[...] / math.sqrt(head_width), 3)
    band = lax.broadcasted_iota(jnp.int32, (3 * HEADS, width), 0) // HEADS
    q_rows = jnp.where(band == 0, q3[0], jnp.where(band == 1, q3[1], q3[2]))
    table = (q_rows * hm[0 : 3 * HEADS, :].astype(F32)).astype(BF16)
    load_k.wait()
    kpt = mm_nt(table, wk[...])
    kp = kpt[0:HEADS] + kpt[HEADS : 2 * HEADS] + kpt[2 * HEADS : 3 * HEADS]
    kp_pieces = pieces(kp, 3)
    kp3[...] = jnp.concatenate(kp_pieces, axis=0).astype(BF16)
    kpr[...] = jnp.zeros_like(kpr)
    kpr[3 * HEADS : 6 * HEADS, :] = jnp.concatenate(
        [kp_pieces[0], kp_pieces[1], kp_pieces[0]], axis=0
    ).astype(BF16)

    pl.semaphore_wait(barrier, nplane - 1 + nq - 1)
    pair = remote(patches, p.at[1], pair_send.at[0], pair_recv.at[0], (blk, sib))
    pair.start()
    t_all[place] = text[...]
    spread(plane_peer, nplane, lambda k: text, t_all, place, text_send, text_recv)

    def project(part):
        s = mm_nt(kp3[...], p[part])
        st[:, part * rows : (part + 1) * rows] = (
            s[0:HEADS] + s[HEADS : 2 * HEADS] + s[2 * HEADS : 3 * HEADS]
        )

        def step(j, carry):
            cols = pl.ds(pl.multiple_of(j * CHUNK, CHUNK), CHUNK)
            v[part, :, cols] = mm(p[part], wv[:, cols])
            return carry

        lax.fori_loop(0, chunks, step, 0)

    load_p.wait()
    load_v.wait()
    project(0)
    own_owner = owner[0, pl.ds(grp, 1), :]
    own_slot = slot[0, pl.ds(grp, 1), :]
    own_id = own_owner * IMG + own_slot
    sib_id = owner[0, pl.ds(sib, 1), :] * IMG + slot[0, pl.ds(sib, 1), :]
    pair.wait_recv()
    project(1)

    ids = jnp.concatenate([own_id, sib_id], axis=1)
    img_i = lax.broadcasted_iota(jnp.int32, (mine, 2 * rows), 0)
    member = ids == (img_i >> 2) * (2 * IMG) + core * IMG + (img_i & (IMG - 1))
    ot[...] = jnp.where(member, 1.0, 0.0).astype(BF16)
    valid = ((ids >> 2) & 1) == core
    scores = st[...]
    lane = lax.broadcasted_iota(jnp.int32, (mine, LANES), 1)
    peak = jnp.zeros((mine, LANES), F32)
    for h in range(HEADS):
        top = jnp.max(jnp.where(member, scores[h : h + 1, :], LOW), axis=1, keepdims=True)
        peak = jnp.where(lane == h, top, peak)
    peak_t = jnp.transpose(peak)[0:HEADS]
    shift = mm(stacked(peak_t, 3), ot[...])
    shift = shift[0:HEADS] + shift[HEADS : 2 * HEADS] + shift[2 * HEADS : 3 * HEADS]
    e = jnp.where(valid, jnp.exp(scores - shift), 0.0)
    e_hi, e_lo = pieces(e, 2)
    e_pad = jnp.concatenate(
        [
            jnp.zeros((HEADS, 2 * rows), F32),
            e_hi,
            e_lo,
            jnp.zeros((LANES - 3 * HEADS, 2 * rows), F32),
        ],
        axis=0,
    )
    et[...] = jnp.transpose(e_pad).astype(BF16)
    stats = jnp.where(lane < HEADS, peak, mm(ot[...], et[...]))
    for k in range(nq):
        acc_out[k, :, width : width + LANES] = stats[k * IMG : (k + 1) * IMG]

    def pool(j, carry):
        cols = pl.ds(pl.multiple_of(j * CHUNK, CHUNK), CHUNK)
        spread_e = mm(et[...], hm[:, cols])
        total = jnp.zeros((mine, CHUNK), F32)
        for part in range(2):
            here = slice(part * rows, (part + 1) * rows)
            x_hi, x_lo = pieces(spread_e[here] * v[part, :, cols], 2)
            total += mm(ot[:, here], x_hi.astype(BF16)) + mm(ot[:, here], x_lo.astype(BF16))
        for k in range(nq):
            acc_out[k, :, cols] = total[k * IMG : (k + 1) * IMG]
        return carry

    lax.fori_loop(0, chunks, pool, 0)
    spread(group_peer, nq, lambda k: acc_out.at[k], acc_in, q, acc_send, acc_recv)
    acc_in[q] = acc_out[q]

    gather_wait(plane_peer, nplane, t_all, text_send, text_recv)
    for k in range(nplane):
        tf[k * IMG : (k + 1) * IMG, :] = t_all[k].astype(F32)
    texts = tf[...]
    tb = texts.astype(BF16)
    inv = 1.0 / jnp.sqrt(jnp.sum(texts * texts, axis=1, keepdims=True) + EPS)
    inv_row = jnp.transpose(jnp.broadcast_to(inv, (nplane * IMG, LANES)))[0:1, :]
    own_code = (own_owner & 1) * mine + (own_owner >> 1) * IMG + own_slot
    code_i = lax.broadcasted_iota(jnp.int32, (2 * mine, rows), 0)
    own_ot = jnp.where(own_code == code_i, 1.0, 0.0)
    own_o = jnp.transpose(own_ot).astype(BF16)
    ob[:, 0 : 2 * mine] = own_o
    ob[:, 2 * mine : 4 * mine] = own_o
    rows16[...] = jnp.zeros_like(rows16)
    load_o.wait()

    gather_wait(group_peer, nq, acc_in, acc_send, acc_recv)
    lane4 = lax.broadcasted_iota(jnp.int32, (IMG, LANES), 1)
    heads4 = lane4 < HEADS
    parts = [acc_in[k, :, width : width + LANES] for k in range(nq)]
    m = parts[0]
    for part in parts[1:]:
        m = jnp.maximum(m, part)
    factors = []
    denom = jnp.zeros((IMG, LANES), F32)
    for part in parts:
        f = jnp.exp(part - m)
        mass = pltpu.roll(part, LANES - HEADS, 1) + pltpu.roll(part, LANES - 2 * HEADS, 1)
        factors.append(f)
        denom = denom + f * mass
    denom = jnp.where(heads4, denom, 1.0)
    lse = m + jnp.log(denom)
    for k, f in enumerate(factors):
        f_hi, f_lo = pieces(jnp.where(heads4, f / denom, 0.0), 2)
        fs[k * IMG : (k + 1) * IMG, :] = f_hi + pltpu.roll(f_lo, HEADS, 1)
    factor = mm(fs[...].astype(BF16), hm[...])
    pooled = jnp.zeros((IMG, width), F32)
    for k in range(nq):
        pooled = pooled + factor[k * IMG : (k + 1) * IMG] * acc_in[k, :, 0:width]
    pooled_buf[...] = pooled
    embeds = three(mm(small_rows(pooled, rows16), wo[...]))
    norm = jnp.sqrt(jnp.sum(embeds * embeds, axis=1, keepdims=True) + EPS)
    unit = embeds / norm
    unit_all[z] = unit
    spread(line_peer, nz, lambda k: unit_all.at[z], unit_all, z, unit_send, unit_recv)

    gather_wait(line_peer, nz, unit_all, unit_send, unit_recv)
    for k in range(nz):
        u32[k * IMG : (k + 1) * IMG, :] = unit_all[k]
    nimg = nz * IMG
    ntext = nplane * IMG
    u_pieces = pieces(u32[...], 3)
    dots = mm_nt(jnp.concatenate(u_pieces, axis=0).astype(BF16), tb)
    dots = dots[0:nimg] + dots[nimg : 2 * nimg] + dots[2 * nimg : 3 * nimg]
    temper = jnp.exp(jnp.full((1, 1), logit_scale[0], F32))
    logits = temper * (dots * inv_row) + logit_bias[0]
    block_row = lax.broadcasted_iota(jnp.int32, (nimg, ntext), 0)
    block_col = lax.broadcasted_iota(jnp.int32, (nimg, ntext), 1)
    positive = ((block_row >> 2) == z) & (block_col - place * IMG == (block_row & (IMG - 1)))
    signal = 1.0 / (1.0 + jnp.exp(-logits)) - jnp.where(positive, 1.0, 0.0)
    di = mm(stacked(signal * inv_row, 3), tb)
    di = di[0:nimg] + di[nimg : 2 * nimg] + di[2 * nimg : 3 * nimg]
    for k in range(nz):
        di_out[k] = di[k * IMG : (k + 1) * IMG]
    spread(line_peer, nz, lambda k: di_out.at[k], di_in, z, di_send, di_recv)
    di_in[z] = di_out[z]

    s_hi, s_lo = pieces(signal, 2)
    s_pad = jnp.concatenate(
        [s_hi, s_hi, s_lo, jnp.zeros((LANES - 3 * nimg, ntext), F32)], axis=0
    )
    s_t = jnp.transpose(s_pad).astype(BF16)
    u_pad = jnp.concatenate(
        [u_pieces[0], u_pieces[1], u_pieces[0], jnp.zeros((LANES - 3 * nimg, width), F32)], axis=0
    ).astype(BF16)
    td = mm(s_t, u_pad)
    for k in range(nplane):
        t_out[k] = td[k * IMG : (k + 1) * IMG]
    spread(plane_peer, nplane, lambda k: t_out.at[k], t_in, place, td_send, td_recv)
    t_in[place] = t_out[place]

    gather_wait(line_peer, nz, di_in, di_send, di_recv)
    dunit = di_in[0]
    for k in range(1, nz):
        dunit = dunit + di_in[k]
    dunit = dunit * (temper * LOSS_SCALE)
    unit = unit_all[z]
    embed_grad = (dunit - unit * jnp.sum(unit * dunit, axis=1, keepdims=True)) / norm
    pooled_grad = three(mm_nt(small_rows(embed_grad, rows16), wo[...]))
    mass = three(mm_nt(small_rows(pooled_grad * pooled_buf[...], rows16), hm[...]))
    pg_all[core, q, :, 0:width] = pooled_grad
    pg_all[core, q, :, width : width + LANES] = jnp.where(
        heads4, lse, jnp.where(lane4 < 2 * HEADS, mass, 0.0)
    )
    own_half = pg_all.at[core]
    spread(group_peer, nq, lambda k: own_half.at[q], own_half, q, pg_send, pg_recv)

    gather_wait(plane_peer, nplane, t_in, td_send, td_recv)
    text_dunit = t_in[0]
    for k in range(1, nplane):
        text_dunit = text_dunit + t_in[k]
    text_dunit = text_dunit * (temper * LOSS_SCALE)
    own_text = text[...].astype(F32)
    text_norm = jnp.sqrt(jnp.sum(own_text * own_text, axis=1, keepdims=True) + EPS)
    text_unit = own_text / text_norm
    g_text[...] = (
        (text_dunit - text_unit * jnp.sum(text_unit * text_dunit, axis=1, keepdims=True))
        / text_norm
    ).astype(BF16)

    gather_wait(group_peer, nq, own_half, pg_send, pg_recv)
    swap = remote(pg_all.at[core], pg_all.at[core], pair_send.at[1], pair_recv.at[1], (blk, sib))
    swap.start()
    swapped = remote(
        pg_all.at[1 - core], pg_all.at[1 - core], pair_send.at[1], pair_recv.at[1], (blk, sib)
    )
    swapped.wait_recv()

    for c in range(2):
        for k in range(nq):
            at = (c * nq + k) * IMG
            pgm[at : at + IMG, :] = pg_all[c, k]
    row_stats = stacked(jnp.transpose(pgm[:, width : width + LANES])[0 : 2 * HEADS], 3)
    row_stats = mm(row_stats, own_ot.astype(BF16))
    row_stats = (
        row_stats[0 : 2 * HEADS] + row_stats[2 * HEADS : 4 * HEADS] + row_stats[4 * HEADS : 6 * HEADS]
    )
    pgr = mm(ob[...], stacked(pgm[:, 0:width], 2))
    d_hi, d_lo = pieces(pgr * v[0], 2)
    dw = mm_nt(hm[0:HEADS, :], d_hi.astype(BF16)) + mm_nt(hm[0:HEADS, :], d_lo.astype(BF16))
    w = jnp.exp(st[:, 0:rows] - row_stats[0:HEADS])
    ds = w * (dw - row_stats[HEADS : 2 * HEADS])
    w_hi, w_lo = pieces(w, 2)
    ds_hi, ds_lo = pieces(ds, 2)
    blank = jnp.zeros((HEADS, rows), F32)
    wt = jnp.transpose(
        jnp.concatenate([w_hi, w_lo, blank, ds_hi, ds_hi, ds_lo, blank, blank], axis=0)
    ).astype(BF16)
    vg[...] = stacked(mm(wt, hm[...]) * pgr, 2)
    et[0:rows, :] = wt

    def back(j, carry):
        cols = pl.ds(pl.multiple_of(j * CHUNK, CHUNK), CHUNK)
        g = mm_nt(vg[...], wv[cols, :])
        g_patch[:, cols] = (g[0:rows] + g[rows : 2 * rows] + mm(et[0:rows, :], kpr[:, cols])).astype(
            BF16
        )
        return carry

    lax.fori_loop(0, chunks, back, 0)

    pair.wait_send()
    swap.wait_send()
    send_wait(plane_peer, nplane, lambda k: text, text_send, text_recv)
    send_wait(group_peer, nq, lambda k: acc_out.at[k], acc_send, acc_recv)
    send_wait(line_peer, nz, lambda k: unit_all.at[z], unit_send, unit_recv)
    send_wait(line_peer, nz, lambda k: di_out.at[k], di_send, di_recv)
    send_wait(plane_peer, nplane, lambda k: t_out.at[k], td_send, td_recv)
    send_wait(group_peer, nq, lambda k: own_half.at[q], pg_send, pg_recv)


def local(nb, ng, nz, patches, owner, slot, text, probe, w_key, w_value, w_out, scale, bias):
    rows, width = patches.shape
    nq = ng // 2
    nplane = nb * (nq // nz) * 2
    mine = nq * IMG
    vmem = pl.BlockSpec(memory_space=pltpu.VMEM)
    smem = pl.BlockSpec(memory_space=pltpu.SMEM)
    anywhere = pl.BlockSpec(memory_space=pl.ANY)
    weight = pltpu.VMEM((width, width), BF16)
    dma = pltpu.SemaphoreType.DMA
    return pl.pallas_call(
        functools.partial(kernel, nb, ng, nz),
        out_shape=(
            jax.ShapeDtypeStruct((rows, width), BF16),
            jax.ShapeDtypeStruct((IMG, width), BF16),
        ),
        in_specs=[anywhere, vmem, vmem, vmem, vmem, anywhere, anywhere, anywhere, smem, smem],
        out_specs=(vmem, vmem),
        scratch_shapes=[
            weight,
            weight,
            weight,
            pltpu.VMEM((2, rows, width), BF16),
            pltpu.VMEM((2, rows, width), F32),
            pltpu.VMEM((HEADS, 2 * rows), F32),
            pltpu.VMEM((LANES, width), BF16),
            pltpu.VMEM((3 * HEADS, width), BF16),
            pltpu.VMEM((LANES, width), BF16),
            pltpu.VMEM((mine, 2 * rows), BF16),
            pltpu.VMEM((2 * rows, LANES), BF16),
            pltpu.VMEM((nq, IMG, width + LANES), F32),
            pltpu.VMEM((nq, IMG, width + LANES), F32),
            pltpu.VMEM((mine, LANES), F32),
            pltpu.VMEM((16, width), F32),
            pltpu.VMEM((IMG, width), F32),
            pltpu.VMEM((nz, IMG, width), F32),
            pltpu.VMEM((nz * IMG, width), F32),
            pltpu.VMEM((nz, IMG, width), F32),
            pltpu.VMEM((nz, IMG, width), F32),
            pltpu.VMEM((nplane, IMG, width), BF16),
            pltpu.VMEM((nplane * IMG, width), F32),
            pltpu.VMEM((nplane, IMG, width), F32),
            pltpu.VMEM((nplane, IMG, width), F32),
            pltpu.VMEM((2, nq, IMG, width + LANES), F32),
            pltpu.VMEM((2 * mine, width + LANES), F32),
            pltpu.VMEM((rows, 4 * mine), BF16),
            pltpu.VMEM((2 * rows, width), BF16),
            dma((4,)),
            dma((2,)),
            dma((2,)),
            dma((nplane,)),
            dma((nplane,)),
            dma((nq,)),
            dma((nq,)),
            dma((nz,)),
            dma((nz,)),
            dma((nz,)),
            dma((nz,)),
            dma((nplane,)),
            dma((nplane,)),
            dma((nq,)),
            dma((nq,)),
        ],
        compiler_params=pltpu.CompilerParams(
            collective_id=0, has_side_effects=True, vmem_limit_bytes=56 * 2**20
        ),
        name="pool_contrast",
    )(patches, owner, slot, text, probe.reshape(1, width), w_key, w_value, w_out, scale, bias)


def solution(mesh):
    nb = mesh.shape["blk"]
    ng = mesh.shape["group"]
    nz = ng // 4
    return jax.shard_map(
        functools.partial(local, nb, ng, nz),
        mesh=mesh,
        in_specs=(
            P(("blk", "group"), None),
            P("blk", None, None),
            P("blk", None, None),
            P(("blk", "group"), None),
            P(),
            P(),
            P(),
            P(),
            P(),
            P(),
        ),
        out_specs=(P(("blk", "group"), None), P(("blk", "group"), None)),
        check_vma=False,
    )
```

time: 596 us -> 68.4 us (0.11); the launches traced: 586 us -> 67.6 us
  waiting for transfers between devices: 318 us -> 0 us
  matrix products: 81.9 us -> 0 us
  blocking collectives: 75.5 us -> 0 us
  Pallas kernels: 0 us -> 61.1 us
  local copies, waits for them, and re-layouts: 60.7 us -> 4.52 us
  starting transfers between devices: 26.9 us -> 0 us
  between operations: 16.3 us -> 1.93 us
  other arithmetic: 7.58 us -> 0 us
    unnamed x2 -> x0, waiting for transfers between devices: 273 us -> none
    dot_general x34 -> x0, matrix products: 81.9 us -> none  [the longest x1 15.7 us: local(): jnp.dot(value_grad, w_value.T, precision=highest, preferred_element_type=...]
    all_gather x1 -> x0, blocking collectives: 75.5 us -> none  [local(): group_texts = lax.all_gather(text_embed, 'group', axis=0, tiled=True)]
    pallas_call x0 -> x1, Pallas kernels: none -> 61.1 us  [local(): pl.pallas_call(functools.partial(kernel, nb, ng, nz), out_shape=(jax.Shap...]
    ppermute x7 -> x0, waiting for transfers between devices: 44.8 us -> none  [passed_along(): return lax.ppermute(block, axis, route)]
    unnamed x53 -> x2, local copies, waits for them, and re-layouts: 34.5 us -> 3.23 us
    all_to_all x2 -> x0, starting transfers between devices: 23.5 us -> none  [the longest x1 12.6 us: local(): lax.all_to_all(outgoing, 'group', split_axis=0, concat_axis=0, tiled=True)]
    reshape x5 -> x1, local copies, waits for them, and re-layouts: 14.2 us -> 1.29 us  [local(): probe.reshape(1, width)]
  transfers between devices with their start and end apart: 10 -> 0, of which waited for: 7 -> 0; matrix products, arithmetic and copies ran while one was open for 9% -> 0% of each run, Pallas kernels for 0% -> 0%
where the time goes in v1:
time: 68.4 us; the launch traced here: 67.6 us
  Pallas kernels  61.1 us (89%)
  local copies, waits for them, and re-layouts  4.52 us (7%)
  between operations  1.93 us (3%)
    pallas_call x1, Pallas kernels, local(): pl.pallas_call(functools.partial(kernel, nb, ng, nz), out_shape=(jax.Shap...  61.1 us
    unnamed x2, local copies, waits for them, and re-layouts  3.23 us

profile of v1, /device:TPU:1, one launch (start us, length us, event | category | flops | bytes accessed | tf_op | source)
XLA Modules:
  0.0 67.6 jit_solution(7796391106350115149)
XLA Ops:
  1.9 1.3 %reshape.7.probe = f32[1,1152]{1,0:T(1,128)} reshape(f32[1152]{0:T(1024)} %param.14) | data formatting | bytes 9216 | tf_op jit(solution)/shard_map/reshape | solution.py:524
  3.2 61.1 %pool_contrast.1 = (bf16[256,1152]{1,0:T(8,128)(2,1)}, bf16[4,1152]{1,0:T(4,128)(2,1)}) custom-call(bf16[256,1152]{1,0:T(8,128)(2,1)} %patches.1, s32[1,32,256]{2,1,0:T(8,128)} %owner.1, s32[1,32,256]{2,1,0:T(8,128)} %slot.1, bf16[4,1152]{1,0:T(4,128)(2,1)} %text.1, f32[1,1152]{1,0:T(1,128)} %reshape.7.probe, bf16[1152,1152]{1,0:T(8,128)(2,1)} %w_key.1, ...), custom_call_target="tpu_custom_call" | custom-call | tf_op jit(solution)/shard_map/pool_contrast/pallas_call | solution.py:467
  64.3 1.9 %copy.16 = bf16[256,1152]{1,0:T(8,128)(2,1)} copy(bf16[256,1152]{1,0:T(8,128)(2,1)} %get-tuple-element.4) | data formatting | bytes 1179648
  66.3 1.3 %copy.17 = bf16[4,1152]{1,0:T(4,128)(2,1)} copy(bf16[4,1152]{1,0:T(4,128)(2,1)} %get-tuple-element.5) | data formatting | bytes 18432

commit v2 on v1

v2 whole, which is shorter than its diff:
```python
import functools
import math

import jax
import jax.numpy as jnp
from jax import lax
from jax.experimental import pallas as pl
from jax.experimental.pallas import tpu as pltpu
from jax.sharding import PartitionSpec as P

HEADS = 16
IMG = 4
X_LOW, X_HIGH = 2, 2
LANES = 128
CHUNK = 384
LOSS_SCALE = 256.0
EPS = 1e-06
LOW = -1e30

F32 = jnp.float32
BF16 = jnp.bfloat16
MESH = pl.DeviceIdType.MESH


def mm(a, b):
    return lax.dot_general(a, b, (((1,), (0,)), ((), ())), preferred_element_type=F32)


def mm_nt(a, b):
    return lax.dot_general(a, b, (((1,), (1,)), ((), ())), preferred_element_type=F32)


def pieces(x, count):
    out = []
    for _ in range(count - 1):
        top = x.astype(BF16).astype(F32)
        out.append(top)
        x = x - top
    out.append(x.astype(BF16).astype(F32))
    return out


def stacked(x, count):
    return jnp.concatenate(pieces(x, count), axis=0).astype(BF16)


def small_rows(x, buf):
    for k, piece in enumerate(pieces(x, 3)):
        buf[k * IMG : (k + 1) * IMG, :] = piece
    return buf[...].astype(BF16)


def three(y):
    return y[0:IMG] + y[IMG : 2 * IMG] + y[2 * IMG : 3 * IMG]


def far(j, n):
    return (n // 2 + ((j + 1) // 2) * (2 * ((j + 1) % 2) - 1)) % n


def kernel(
    nb,
    ng,
    patches,
    owner_in,
    slot_in,
    text_in,
    probe,
    w_key,
    w_value,
    w_out,
    logit_scale,
    logit_bias,
    g_patch,
    g_text,
    owner,
    slot,
    text,
    wk,
    wv,
    wo,
    p,
    v,
    st,
    hm,
    kp3,
    kpr,
    ot,
    et,
    part_own,
    part_in,
    acc_out,
    acc_in,
    fs,
    rows16,
    pooled_buf,
    unit_line,
    u16,
    di_out,
    di_in,
    unit_all,
    u64,
    t_img,
    tf,
    t_txt,
    tt,
    td_out,
    td_in,
    pg_all,
    pgm,
    vg,
    load_sem,
    pair_send,
    pair_recv,
    tz_send,
    tz_recv,
    tx_send,
    tx_recv,
    tp_send,
    tp_recv,
    acc_send,
    acc_recv,
    uy_send,
    uy_recv,
    uz_send,
    uz_recv,
    di_send,
    di_recv,
    td_send,
    td_recv,
    pg_send,
    pg_recv,
    fw_send,
    fw_recv,
):
    nq = ng // 2
    nz = nq // X_HIGH
    nx = X_LOW * X_HIGH
    ny = nb // X_LOW
    nxy = nx * ny
    mine = nq * IMG
    rows, width = patches.shape
    chunks = width // CHUNK
    head_width = width // HEADS
    blk = lax.axis_index("blk")
    grp = lax.axis_index("group")
    core = grp % 2
    q = grp // 2
    z = q % nz
    xh = q // nz
    y = blk // X_LOW
    x = xh * X_LOW + blk % X_LOW
    xy = y * nx + x
    pending = []

    def at(x_, y_, z_, c_):
        return (y_ * X_LOW + x_ % X_LOW, ((x_ // X_LOW) * nz + z_) * 2 + c_)

    sibling = at(x, y, z, 1 - core)

    def group_peer(i):
        k = ((xh + far(i // nz, X_HIGH)) % X_HIGH) * nz + (z + far(i % nz, nz)) % nz
        return k, (blk, k * 2 + core)

    def z_peer(i):
        k = (z + far(i, nz)) % nz
        return k, at(x, y, k, core)

    def x_peer(i):
        k = (x + far(i, nx)) % nx
        return k, at(k, y, z, core)

    def y_peer(i):
        k = (y + far(i, ny)) % ny
        return k, at(x, k, z, core)

    def plane_peer(i):
        y_ = (y + far(i // nx, ny)) % ny
        x_ = (x + far(i % nx, nx)) % nx
        return y_ * nx + x_, at(x_, y_, z, core)

    def remote(src, dst, send, recv, device):
        return pltpu.make_async_remote_copy(
            src_ref=src,
            dst_ref=dst,
            send_sem=send,
            recv_sem=recv,
            device_id=device,
            device_id_type=MESH,
        )

    def each(count, act):
        def step(i, carry):
            act(i)
            return carry

        lax.fori_loop(0, count - 1, step, 0)

    def spread(peer, count, src_of, dst_of, me, send, recv):
        def act(i):
            k, device = peer(i)
            remote(src_of(k), dst_of(me), send.at[k], recv.at[me], device).start()

        each(count, act)

        def settle(i):
            k, device = peer(i)
            remote(src_of(k), src_of(k), send.at[k], recv.at[k], device).wait_send()

        pending.append(lambda: each(count, settle))

    def gather_wait(peer, count, dst_of, send, recv, then=None):
        def act(i):
            k, device = peer(count - 2 - i)
            remote(dst_of(k), dst_of(k), send.at[k], recv.at[k], device).wait_recv()
            if then is not None:
                then(k)

        each(count, act)

    def to_sibling(src, dst, n):
        copy = remote(src, dst, pair_send.at[n], pair_recv.at[n], sibling)
        copy.start()
        pending.append(copy.wait_send)

    def from_sibling(dst, n):
        remote(dst, dst, pair_send.at[n], pair_recv.at[n], sibling).wait_recv()

    barrier = pltpu.get_barrier_semaphore()

    def greet(peer):
        def act(i):
            pl.semaphore_signal(barrier, inc=1, device_id=peer(i)[1], device_id_type=MESH)

        return act

    each(nq, greet(group_peer))
    each(nxy, greet(plane_peer))
    pl.semaphore_signal(barrier, inc=1, device_id=sibling, device_id_type=MESH)

    loads = [
        pltpu.make_async_copy(src, dst, load_sem.at[n])
        for n, (src, dst) in enumerate(
            [
                (w_key, wk),
                (owner_in, owner),
                (slot_in, slot),
                (patches, p),
                (w_value, wv),
                (text_in, text),
                (w_out, wo),
            ]
        )
    ]
    for load in loads:
        load.start()

    row_i = lax.broadcasted_iota(jnp.int32, (LANES, width), 0)
    col_i = lax.broadcasted_iota(jnp.int32, (LANES, width), 1)
    first = (row_i & (HEADS - 1)) * head_width
    in_head = (col_i >= first) & (col_i < first + head_width)
    hm[...] = jnp.where(in_head & (row_i < 3 * HEADS), 1.0, 0.0).astype(BF16)
    q3 = pieces(probe[...].reshape(1, width) / math.sqrt(head_width), 3)
    band = lax.broadcasted_iota(jnp.int32, (3 * HEADS, width), 0) // HEADS
    q_rows = jnp.where(band == 0, q3[0], jnp.where(band == 1, q3[1], q3[2]))
    table = (q_rows * hm[0 : 3 * HEADS, :].astype(F32)).astype(BF16)
    loads[0].wait()
    kpt = mm_nt(table, wk[...])
    kp = kpt[0:HEADS] + kpt[HEADS : 2 * HEADS] + kpt[2 * HEADS : 3 * HEADS]
    kp_pieces = pieces(kp, 3)
    kp3[...] = jnp.concatenate(kp_pieces, axis=0).astype(BF16)
    kpr[...] = jnp.zeros_like(kpr)
    kpr[3 * HEADS : 6 * HEADS, :] = jnp.concatenate(
        [kp_pieces[0], kp_pieces[1], kp_pieces[0]], axis=0
    ).astype(BF16)
    rows16[...] = jnp.zeros_like(rows16)
    tt[...] = jnp.zeros_like(tt)

    loads[1].wait()
    loads[2].wait()
    own_owner = owner[0, pl.ds(grp, 1), :]
    code = (own_owner & 1) * mine + (own_owner >> 1) * IMG + slot[0, pl.ds(grp, 1), :]
    member = code == lax.broadcasted_iota(jnp.int32, (2 * mine, rows), 0)
    ot_f = jnp.where(member, 1.0, 0.0)
    ot[...] = ot_f.astype(BF16)

    loads[3].wait()
    s = mm_nt(kp3[...], p[...])
    scores = s[0:HEADS] + s[HEADS : 2 * HEADS] + s[2 * HEADS : 3 * HEADS]
    st[...] = scores
    lane = lax.broadcasted_iota(jnp.int32, (2 * mine, LANES), 1)
    peak = jnp.zeros((2 * mine, LANES), F32)
    for h in range(HEADS):
        top = jnp.max(jnp.where(member, scores[h : h + 1, :], LOW), axis=1, keepdims=True)
        peak = jnp.where(lane == h, top, peak)
    peak_t = jnp.transpose(peak)[0:HEADS]
    shift = mm(stacked(peak_t, 3), ot[...])
    shift = shift[0:HEADS] + shift[HEADS : 2 * HEADS] + shift[2 * HEADS : 3 * HEADS]
    e_hi, e_lo = pieces(jnp.exp(scores - shift), 2)
    blank = jnp.zeros((HEADS, rows), F32)
    e_pad = jnp.concatenate(
        [blank, e_hi, e_lo, jnp.zeros((LANES - 3 * HEADS, rows), F32)], axis=0
    )
    et[...] = jnp.transpose(e_pad).astype(BF16)
    stats = jnp.where(lane < HEADS, peak, mm(ot[...], et[...]))
    for c in range(2):
        part_own[c, :, width : width + LANES] = stats[c * mine : (c + 1) * mine]
    loads[4].wait()

    def pool(j, carry):
        cols = pl.ds(pl.multiple_of(j * CHUNK, CHUNK), CHUNK)
        value = mm(p[...], wv[:, cols])
        v[:, cols] = value
        x_hi, x_lo = pieces(mm(et[...], hm[:, cols]) * value, 2)
        total = mm(ot[...], x_hi.astype(BF16)) + mm(ot[...], x_lo.astype(BF16))
        for c in range(2):
            part_own[c, :, cols] = total[c * mine : (c + 1) * mine]
        return carry

    lax.fori_loop(0, chunks, pool, 0)
    loads[5].wait()
    t_img[(core * nx + x) * nz + z] = text[...]
    t_txt[xy] = text[...]

    pl.semaphore_wait(barrier, nq - 1 + nxy - 1 + 1)
    to_sibling(part_own.at[1 - core], part_in, 0)
    z_slab = lambda k: t_img.at[(core * nx + x) * nz + k]
    spread(z_peer, nz, lambda k: text, z_slab, z, tz_send, tz_recv)
    spread(plane_peer, nxy, lambda k: text, lambda k: t_txt.at[k], xy, tp_send, tp_recv)

    from_sibling(part_in, 0)
    lane_m = lax.broadcasted_iota(jnp.int32, (mine, LANES), 1)
    stat_a = part_own[core, :, width : width + LANES]
    stat_b = part_in[:, width : width + LANES]
    top = jnp.maximum(stat_a, stat_b)
    chip_stats = jnp.where(lane_m < HEADS, top, 0.0)
    scale = []
    for stat in (stat_a, stat_b):
        f = jnp.where(lane_m < HEADS, jnp.exp(stat - top), 0.0)
        chip_stats += stat * (pltpu.roll(f, HEADS, 1) + pltpu.roll(f, 2 * HEADS, 1))
        f_hi, f_lo = pieces(f, 2)
        scale.append((f_hi + pltpu.roll(f_lo, HEADS, 1)).astype(BF16))
    for k in range(nq):
        acc_out[k, :, width : width + LANES] = chip_stats[k * IMG : (k + 1) * IMG]
    for j in range(chunks):
        cols = slice(j * CHUNK, (j + 1) * CHUNK)
        total = (
            mm(scale[0], hm[:, cols]) * part_own[core, :, cols]
            + mm(scale[1], hm[:, cols]) * part_in[:, cols]
        )
        for k in range(nq):
            acc_out[k, :, cols] = total[k * IMG : (k + 1) * IMG]
    acc_slab = lambda k: acc_in.at[k]
    spread(group_peer, nq, lambda k: acc_out.at[k], acc_slab, q, acc_send, acc_recv)
    acc_in[q] = acc_out[q]

    gather_wait(z_peer, nz, z_slab, tz_send, tz_recv)
    x_slabs = lambda k: t_img.at[pl.ds((core * nx + k) * nz, nz)]
    spread(x_peer, nx, lambda k: x_slabs(x), x_slabs, x, tx_send, tx_recv)
    gather_wait(plane_peer, nxy, lambda k: t_txt.at[k], tp_send, tp_recv)
    for k in range(nxy):
        tt[k * IMG : (k + 1) * IMG, :] = t_txt[k].astype(F32)
    tt_b = tt[...].astype(BF16)
    tt_inv = 1.0 / jnp.sqrt(jnp.sum(tt[...] * tt[...], axis=1, keepdims=True) + EPS)
    tt_inv = jnp.transpose(jnp.broadcast_to(tt_inv, (LANES, LANES)))[0:1, :]
    gather_wait(x_peer, nx, x_slabs, tx_send, tx_recv)
    t_half = lambda c: t_img.at[pl.ds(c * nx * nz, nx * nz)]
    to_sibling(t_half(core), t_half(core), 1)
    loads[6].wait()

    gather_wait(group_peer, nq, acc_slab, acc_send, acc_recv)
    lane4 = lax.broadcasted_iota(jnp.int32, (IMG, LANES), 1)
    heads4 = lane4 < HEADS
    parts = [acc_in[k, :, width : width + LANES] for k in range(nq)]
    m = parts[0]
    for part in parts[1:]:
        m = jnp.maximum(m, part)
    factors = []
    denom = jnp.zeros((IMG, LANES), F32)
    for part in parts:
        f = jnp.exp(part - m)
        mass = pltpu.roll(part, LANES - HEADS, 1) + pltpu.roll(part, LANES - 2 * HEADS, 1)
        factors.append(f)
        denom = denom + f * mass
    denom = jnp.where(heads4, denom, 1.0)
    lse = m + jnp.log(denom)
    for k, f in enumerate(factors):
        f_hi, f_lo = pieces(jnp.where(heads4, f / denom, 0.0), 2)
        fs[k * IMG : (k + 1) * IMG, :] = f_hi + pltpu.roll(f_lo, HEADS, 1)
    factor = mm(fs[...].astype(BF16), hm[...])
    pooled = jnp.zeros((IMG, width), F32)
    for k in range(nq):
        pooled = pooled + factor[k * IMG : (k + 1) * IMG] * acc_in[k, :, 0:width]
    pooled_buf[...] = pooled
    embeds = three(mm(small_rows(pooled, rows16), wo[...]))
    norm = jnp.sqrt(jnp.sum(embeds * embeds, axis=1, keepdims=True) + EPS)
    unit = embeds / norm
    unit_line[y] = unit
    unit_all[core, z] = unit
    y_slab = lambda k: unit_line.at[k]
    spread(y_peer, ny, lambda k: unit_line.at[y], y_slab, y, uy_send, uy_recv)
    u_slab = lambda k: unit_all.at[core, k]
    spread(z_peer, nz, lambda k: unit_all.at[core, z], u_slab, z, uz_send, uz_recv)

    from_sibling(t_half(1 - core), 1)
    ntext = 2 * nx * nz * IMG
    for k in range(2 * nx * nz):
        tf[k * IMG : (k + 1) * IMG, :] = t_img[k].astype(F32)
    texts = tf[...]
    tb = texts.astype(BF16)
    inv = 1.0 / jnp.sqrt(jnp.sum(texts * texts, axis=1, keepdims=True) + EPS)
    inv_row = jnp.transpose(jnp.broadcast_to(inv, (ntext, LANES)))[0:1, :]
    temper = jnp.exp(jnp.full((1, 1), logit_scale[0], F32))

    def block_signal(u_pieces, tb_, inv_, image_slab, text_slab):
        n, t = u_pieces[0].shape[0], tb_.shape[0]
        dots = mm_nt(jnp.concatenate(u_pieces, axis=0).astype(BF16), tb_)
        dots = dots[0:n] + dots[n : 2 * n] + dots[2 * n : 3 * n]
        logits = temper * (dots * inv_) + logit_bias[0]
        row = lax.broadcasted_iota(jnp.int32, (n, t), 0)
        col = lax.broadcasted_iota(jnp.int32, (n, t), 1)
        positive = ((row >> 2) == image_slab) & (col - text_slab * IMG == (row & (IMG - 1)))
        return 1.0 / (1.0 + jnp.exp(-logits)) - jnp.where(positive, 1.0, 0.0)

    gather_wait(y_peer, ny, y_slab, uy_send, uy_recv)
    nline = ny * IMG
    for k in range(ny):
        u16[k * IMG : (k + 1) * IMG, :] = unit_line[k]
    signal = block_signal(pieces(u16[...], 3), tb, inv_row, y, (core * nx + x) * nz + z)
    di = mm(stacked(signal * inv_row, 3), tb)
    di = di[0:nline] + di[nline : 2 * nline] + di[2 * nline : 3 * nline]
    for k in range(ny):
        di_out[k] = di[k * IMG : (k + 1) * IMG]
    di_slab = lambda k: di_in.at[k]
    spread(y_peer, ny, lambda k: di_out.at[k], di_slab, y, di_send, di_recv)
    di_in[y] = di_out[y]

    gather_wait(z_peer, nz, u_slab, uz_send, uz_recv)
    to_sibling(unit_all.at[core], unit_all.at[core], 2)
    from_sibling(unit_all.at[1 - core], 2)
    for c in range(2):
        for k in range(nz):
            r = (c * nz + k) * IMG
            u64[r : r + IMG, :] = unit_all[c, k]
    u_pieces = pieces(u64[...], 3)
    s_hi, s_lo = pieces(block_signal(u_pieces, tt_b, tt_inv, core * nz + z, xy), 2)
    gap = -6 * nz * IMG % LANES
    s_pad = jnp.concatenate([s_hi, s_hi, s_lo, jnp.zeros((gap, LANES), F32)], axis=0)
    u_pad = jnp.concatenate(
        [u_pieces[0], u_pieces[1], u_pieces[0], jnp.zeros((gap, width), F32)], axis=0
    )
    td = mm(jnp.transpose(s_pad).astype(BF16), u_pad.astype(BF16))
    for k in range(nxy):
        td_out[k] = td[k * IMG : (k + 1) * IMG]
    td_slab = lambda k: td_in.at[k]
    spread(plane_peer, nxy, lambda k: td_out.at[k], td_slab, xy, td_send, td_recv)
    td_in[xy] = td_out[xy]

    gather_wait(y_peer, ny, di_slab, di_send, di_recv)
    dunit = di_in[0]
    for k in range(1, ny):
        dunit = dunit + di_in[k]
    dunit = dunit * (temper * LOSS_SCALE)
    unit = unit_line[y]
    embed_grad = (dunit - unit * jnp.sum(unit * dunit, axis=1, keepdims=True)) / norm
    pooled_grad = three(mm_nt(small_rows(embed_grad, rows16), wo[...]))
    mass = three(mm_nt(small_rows(pooled_grad * pooled_buf[...], rows16), hm[...]))
    pg_all[core, q, :, 0:width] = pooled_grad
    pg_all[core, q, :, width : width + LANES] = jnp.where(
        heads4, lse, jnp.where(lane4 < 2 * HEADS, mass, 0.0)
    )
    pg_slab = lambda k: pg_all.at[core, k]
    spread(group_peer, nq, lambda k: pg_slab(q), pg_slab, q, pg_send, pg_recv)

    def forward(k):
        remote(pg_slab(k), pg_slab(k), fw_send.at[k], fw_recv.at[k], sibling).start()

    forward(q)
    gather_wait(group_peer, nq, pg_slab, pg_send, pg_recv, forward)
    for k in range(nq):
        pgm[core, k * IMG : (k + 1) * IMG, :] = pg_all[core, k]

    gather_wait(plane_peer, nxy, td_slab, td_send, td_recv)
    text_dunit = td_in[0]
    for k in range(1, nxy):
        text_dunit = text_dunit + td_in[k]
    text_dunit = text_dunit * (temper * LOSS_SCALE)
    own_text = text[...].astype(F32)
    text_norm = jnp.sqrt(jnp.sum(own_text * own_text, axis=1, keepdims=True) + EPS)
    text_unit = own_text / text_norm
    g_text[...] = (
        (text_dunit - text_unit * jnp.sum(text_unit * text_dunit, axis=1, keepdims=True))
        / text_norm
    ).astype(BF16)

    def arrived(k, carry):
        other = pg_all.at[1 - core, k]
        remote(other, other, fw_send.at[k], fw_recv.at[k], sibling).wait_recv()
        return carry

    lax.fori_loop(0, nq, arrived, 0)
    for k in range(nq):
        pgm[1 - core, k * IMG : (k + 1) * IMG, :] = pg_all[1 - core, k]
    row_stats = jnp.concatenate([pgm[0, :, width:], pgm[1, :, width:]], axis=0)
    row_stats = mm(stacked(jnp.transpose(row_stats)[0 : 2 * HEADS], 3), ot[...])
    row_stats = (
        row_stats[0 : 2 * HEADS] + row_stats[2 * HEADS : 4 * HEADS] + row_stats[4 * HEADS : 6 * HEADS]
    )
    own_o = jnp.transpose(jnp.concatenate([ot_f, ot_f], axis=0)).astype(BF16)
    pg = jnp.concatenate([pgm[0, :, 0:width], pgm[1, :, 0:width]], axis=0)
    pgr = mm(own_o, stacked(pg, 2))
    d_hi, d_lo = pieces(pgr * v[...], 2)
    dw = mm_nt(hm[0:HEADS, :], d_hi.astype(BF16)) + mm_nt(hm[0:HEADS, :], d_lo.astype(BF16))
    w = jnp.exp(st[...] - row_stats[0:HEADS])
    ds = w * (dw - row_stats[HEADS : 2 * HEADS])
    w_hi, w_lo = pieces(w, 2)
    ds_hi, ds_lo = pieces(ds, 2)
    wt = jnp.transpose(
        jnp.concatenate([w_hi, w_lo, blank, ds_hi, ds_hi, ds_lo, blank, blank], axis=0)
    ).astype(BF16)
    vg[...] = stacked(mm(wt, hm[...]) * pgr, 2)
    et[...] = wt

    def back(j, carry):
        cols = pl.ds(pl.multiple_of(j * CHUNK, CHUNK), CHUNK)
        g = mm_nt(vg[...], wv[cols, :])
        g_patch[:, cols] = (g[0:rows] + g[rows : 2 * rows] + mm(et[...], kpr[:, cols])).astype(BF16)
        return carry

    lax.fori_loop(0, chunks, back, 0)

    def forwarded(k, carry):
        remote(pg_slab(k), pg_slab(k), fw_send.at[k], fw_recv.at[k], sibling).wait_send()
        return carry

    lax.fori_loop(0, nq, forwarded, 0)
    for settle in pending:
        settle()


def local(nb, ng, patches, owner, slot, text, probe, w_key, w_value, w_out, scale, bias):
    rows, width = patches.shape
    nq = ng // 2
    nz = nq // X_HIGH
    nx = X_LOW * X_HIGH
    ny = nb // X_LOW
    nxy = nx * ny
    mine = nq * IMG
    wide = width + LANES
    vmem = pl.BlockSpec(memory_space=pltpu.VMEM)
    smem = pl.BlockSpec(memory_space=pltpu.SMEM)
    anywhere = pl.BlockSpec(memory_space=pl.ANY)
    weight = pltpu.VMEM((width, width), BF16)
    dma = pltpu.SemaphoreType.DMA
    two = lambda n: [dma((n,)), dma((n,))]
    return pl.pallas_call(
        functools.partial(kernel, nb, ng),
        out_shape=(
            jax.ShapeDtypeStruct((rows, width), BF16),
            jax.ShapeDtypeStruct((IMG, width), BF16),
        ),
        in_specs=[anywhere] * 4 + [vmem] + [anywhere] * 3 + [smem, smem],
        out_specs=(vmem, vmem),
        scratch_shapes=[
            pltpu.VMEM(owner.shape, jnp.int32),
            pltpu.VMEM(slot.shape, jnp.int32),
            pltpu.VMEM(text.shape, BF16),
            weight,
            weight,
            weight,
            pltpu.VMEM((rows, width), BF16),
            pltpu.VMEM((rows, width), F32),
            pltpu.VMEM((HEADS, rows), F32),
            pltpu.VMEM((LANES, width), BF16),
            pltpu.VMEM((3 * HEADS, width), BF16),
            pltpu.VMEM((LANES, width), BF16),
            pltpu.VMEM((2 * mine, rows), BF16),
            pltpu.VMEM((rows, LANES), BF16),
            pltpu.VMEM((2, mine, wide), F32),
            pltpu.VMEM((mine, wide), F32),
            pltpu.VMEM((nq, IMG, wide), F32),
            pltpu.VMEM((nq, IMG, wide), F32),
            pltpu.VMEM((mine, LANES), F32),
            pltpu.VMEM((16, width), F32),
            pltpu.VMEM((IMG, width), F32),
            pltpu.VMEM((ny, IMG, width), F32),
            pltpu.VMEM((ny * IMG, width), F32),
            pltpu.VMEM((ny, IMG, width), F32),
            pltpu.VMEM((ny, IMG, width), F32),
            pltpu.VMEM((2, nz, IMG, width), F32),
            pltpu.VMEM((2 * nz * IMG, width), F32),
            pltpu.VMEM((2 * nx * nz, IMG, width), BF16),
            pltpu.VMEM((2 * nx * nz * IMG, width), F32),
            pltpu.VMEM((nxy, IMG, width), BF16),
            pltpu.VMEM((LANES, width), F32),
            pltpu.VMEM((nxy, IMG, width), F32),
            pltpu.VMEM((nxy, IMG, width), F32),
            pltpu.VMEM((2, nq, IMG, wide), F32),
            pltpu.VMEM((2, mine, wide), F32),
            pltpu.VMEM((2 * rows, width), BF16),
            dma((7,)),
            *two(3),
            *two(nz),
            *two(nx),
            *two(nxy),
            *two(nq),
            *two(ny),
            *two(nz),
            *two(ny),
            *two(nxy),
            *two(nq),
            *two(nq),
        ],
        compiler_params=pltpu.CompilerParams(
            collective_id=0, has_side_effects=True, vmem_limit_bytes=56 * 2**20
        ),
        name="pool_contrast",
    )(patches, owner, slot, text, probe, w_key, w_value, w_out, scale, bias)


def solution(mesh):
    nb = mesh.shape["blk"]
    ng = mesh.shape["group"]
    return jax.shard_map(
        functools.partial(local, nb, ng),
        mesh=mesh,
        in_specs=(
            P(("blk", "group"), None),
            P("blk", None, None),
            P("blk", None, None),
            P(("blk", "group"), None),
            P(),
            P(),
            P(),
            P(),
            P(),
            P(),
        ),
        out_specs=(P(("blk", "group"), None), P(("blk", "group"), None)),
        check_vma=False,
    )
```

time: 68.4 us -> 63.2 us (0.924)
  Pallas kernels: 61.1 us -> 57.8 us
  local copies, waits for them, and re-layouts: 4.52 us -> 3.23 us
    pallas_call x1, Pallas kernels: 61.1 us -> 57.8 us  [local(): pl.pallas_call(functools.partial(kernel, nb, ng), out_shape=(jax.ShapeDty...]
    reshape x1 -> x0, local copies, waits for them, and re-layouts: 1.29 us -> none  [local(): probe.reshape(1, width)]
where the time goes in v2:
time: 63.2 us; the launch traced here: 63 us
  Pallas kernels  57.8 us (91%)
  local copies, waits for them, and re-layouts  3.23 us (5%)
  between operations  1.93 us (3%)
    pallas_call x1, Pallas kernels, local(): pl.pallas_call(functools.partial(kernel, nb, ng), out_shape=(jax.ShapeDty...  57.8 us
    unnamed x2, local copies, waits for them, and re-layouts  3.23 us

profile of v2, /device:TPU:1, one launch (start us, length us, event | category | flops | bytes accessed | tf_op | source)
XLA Modules:
  0.0 63.0 jit_solution(14693101526400399245)
XLA Ops:
  1.9 57.8 %pool_contrast.1 = (bf16[256,1152]{1,0:T(8,128)(2,1)}, bf16[4,1152]{1,0:T(4,128)(2,1)}) custom-call(bf16[256,1152]{1,0:T(8,128)(2,1)} %patches.1, s32[1,32,256]{2,1,0:T(8,128)} %owner_in.1, s32[1,32,256]{2,1,0:T(8,128)} %slot_in.1, bf16[4,1152]{1,0:T(4,128)(2,1)} %text_in.1, f32[1152]{0:T(1024)} %probe.1, bf16[1152,1152]{1,0:T(8,128)(2,1)} %w_key.1, ...), custom_call_target="tpu_custom_call" | custom-call | tf_op jit(solution)/shard_map/pool_contrast/pallas_call | solution.py:556
  59.8 1.9 %copy.16 = bf16[256,1152]{1,0:T(8,128)(2,1)} copy(bf16[256,1152]{1,0:T(8,128)(2,1)} %get-tuple-element.4) | data formatting | bytes 1179648
  61.7 1.3 %copy.17 = bf16[4,1152]{1,0:T(4,128)(2,1)} copy(bf16[4,1152]{1,0:T(4,128)(2,1)} %get-tuple-element.5) | data formatting | bytes 18432

commit v3 on v2

--- a/solution.py
+++ b/solution.py
@@ -324,9 +324,6 @@
 
     pl.semaphore_wait(barrier, nq - 1 + nxy - 1 + 1)
     to_sibling(part_own.at[1 - core], part_in, 0)
-    z_slab = lambda k: t_img.at[(core * nx + x) * nz + k]
-    spread(z_peer, nz, lambda k: text, z_slab, z, tz_send, tz_recv)
-    spread(plane_peer, nxy, lambda k: text, lambda k: t_txt.at[k], xy, tp_send, tp_recv)
 
     from_sibling(part_in, 0)
     lane_m = lax.broadcasted_iota(jnp.int32, (mine, LANES), 1)
@@ -352,8 +349,10 @@
             acc_out[k, :, cols] = total[k * IMG : (k + 1) * IMG]
     acc_slab = lambda k: acc_in.at[k]
     spread(group_peer, nq, lambda k: acc_out.at[k], acc_slab, q, acc_send, acc_recv)
+    z_slab = lambda k: t_img.at[(core * nx + x) * nz + k]
+    spread(z_peer, nz, lambda k: text, z_slab, z, tz_send, tz_recv)
+    spread(plane_peer, nxy, lambda k: text, lambda k: t_txt.at[k], xy, tp_send, tp_recv)
     acc_in[q] = acc_out[q]
-
     gather_wait(z_peer, nz, z_slab, tz_send, tz_recv)
     x_slabs = lambda k: t_img.at[pl.ds((core * nx + k) * nz, nz)]
     spread(x_peer, nx, lambda k: x_slabs(x), x_slabs, x, tx_send, tx_recv)
@@ -435,6 +434,27 @@
     spread(y_peer, ny, lambda k: di_out.at[k], di_slab, y, di_send, di_recv)
     di_in[y] = di_out[y]
 
+    gather_wait(y_peer, ny, di_slab, di_send, di_recv)
+    dunit = di_in[0]
+    for k in range(1, ny):
+        dunit = dunit + di_in[k]
+    dunit = dunit * (temper * LOSS_SCALE)
+    unit = unit_line[y]
+    embed_grad = (dunit - unit * jnp.sum(unit * dunit, axis=1, keepdims=True)) / norm
+    pooled_grad = three(mm_nt(small_rows(embed_grad, rows16), wo[...]))
+    mass = three(mm_nt(small_rows(pooled_grad * pooled_buf[...], rows16), hm[...]))
+    pg_all[core, q, :, 0:width] = pooled_grad
+    pg_all[core, q, :, width : width + LANES] = jnp.where(
+        heads4, lse, jnp.where(lane4 < 2 * HEADS, mass, 0.0)
+    )
+    pg_slab = lambda k: pg_all.at[core, k]
+    spread(group_peer, nq, lambda k: pg_slab(q), pg_slab, q, pg_send, pg_recv)
+
+    def forward(k):
+        remote(pg_slab(k), pg_slab(k), fw_send.at[k], fw_recv.at[k], sibling).start()
+
+    forward(q)
+
     gather_wait(z_peer, nz, u_slab, uz_send, uz_recv)
     to_sibling(unit_all.at[core], unit_all.at[core], 2)
     from_sibling(unit_all.at[1 - core], 2)
@@ -456,42 +476,9 @@
     spread(plane_peer, nxy, lambda k: td_out.at[k], td_slab, xy, td_send, td_recv)
     td_in[xy] = td_out[xy]
 
-    gather_wait(y_peer, ny, di_slab, di_send, di_recv)
-    dunit = di_in[0]
-    for k in range(1, ny):
-        dunit = dunit + di_in[k]
-    dunit = dunit * (temper * LOSS_SCALE)
-    unit = unit_line[y]
-    embed_grad = (dunit - unit * jnp.sum(unit * dunit, axis=1, keepdims=True)) / norm
-    pooled_grad = three(mm_nt(small_rows(embed_grad, rows16), wo[...]))
-    mass = three(mm_nt(small_rows(pooled_grad * pooled_buf[...], rows16), hm[...]))
-    pg_all[core, q, :, 0:width] = pooled_grad
-    pg_all[core, q, :, width : width + LANES] = jnp.where(
-        heads4, lse, jnp.where(lane4 < 2 * HEADS, mass, 0.0)
-    )
-    pg_slab = lambda k: pg_all.at[core, k]
-    spread(group_peer, nq, lambda k: pg_slab(q), pg_slab, q, pg_send, pg_recv)
-
-    def forward(k):
-        remote(pg_slab(k), pg_slab(k), fw_send.at[k], fw_recv.at[k], sibling).start()
-
-    forward(q)
     gather_wait(group_peer, nq, pg_slab, pg_send, pg_recv, forward)
     for k in range(nq):
         pgm[core, k * IMG : (k + 1) * IMG, :] = pg_all[core, k]
-
-    gather_wait(plane_peer, nxy, td_slab, td_send, td_recv)
-    text_dunit = td_in[0]
-    for k in range(1, nxy):
-        text_dunit = text_dunit + td_in[k]
-    text_dunit = text_dunit * (temper * LOSS_SCALE)
-    own_text = text[...].astype(F32)
-    text_norm = jnp.sqrt(jnp.sum(own_text * own_text, axis=1, keepdims=True) + EPS)
-    text_unit = own_text / text_norm
-    g_text[...] = (
-        (text_dunit - text_unit * jnp.sum(text_unit * text_dunit, axis=1, keepdims=True))
-        / text_norm
-    ).astype(BF16)
 
     def arrived(k, carry):
         other = pg_all.at[1 - core, k]
@@ -529,6 +516,19 @@
 
     lax.fori_loop(0, chunks, back, 0)
 
+    gather_wait(plane_peer, nxy, td_slab, td_send, td_recv)
+    text_dunit = td_in[0]
+    for k in range(1, nxy):
+        text_dunit = text_dunit + td_in[k]
+    text_dunit = text_dunit * (temper * LOSS_SCALE)
+    own_text = text[...].astype(F32)
+    text_norm = jnp.sqrt(jnp.sum(own_text * own_text, axis=1, keepdims=True) + EPS)
+    text_unit = own_text / text_norm
+    g_text[...] = (
+        (text_dunit - text_unit * jnp.sum(text_unit * text_dunit, axis=1, keepdims=True))
+        / text_norm
+    ).astype(BF16)
+
     def forwarded(k, carry):
         remote(pg_slab(k), pg_slab(k), fw_send.at[k], fw_recv.at[k], sibling).wait_send()
         return carry
@@ -536,6 +536,17 @@
     lax.fori_loop(0, nq, forwarded, 0)
     for settle in pending:
         settle()
+
+
+def hand_over(patch_in, text_in, patch_out, text_out, sem):
+    copies = [
+        pltpu.make_async_copy(patch_in, patch_out, sem.at[0]),
+        pltpu.make_async_copy(text_in, text_out, sem.at[1]),
+    ]
+    for copy in copies:
+        copy.start()
+    for copy in copies:
+        copy.wait()
 
 
 def local(nb, ng, patches, owner, slot, text, probe, w_key, w_value, w_out, scale, bias):
@@ -548,17 +559,18 @@
     mine = nq * IMG
     wide = width + LANES
     vmem = pl.BlockSpec(memory_space=pltpu.VMEM)
+    anywhere = pl.BlockSpec(memory_space=pl.ANY)
     smem = pl.BlockSpec(memory_space=pltpu.SMEM)
-    anywhere = pl.BlockSpec(memory_space=pl.ANY)
     weight = pltpu.VMEM((width, width), BF16)
     dma = pltpu.SemaphoreType.DMA
     two = lambda n: [dma((n,)), dma((n,))]
-    return pl.pallas_call(
+    shapes = (
+        jax.ShapeDtypeStruct((rows, width), BF16),
+        jax.ShapeDtypeStruct((IMG, width), BF16),
+    )
+    grads = pl.pallas_call(
         functools.partial(kernel, nb, ng),
-        out_shape=(
-            jax.ShapeDtypeStruct((rows, width), BF16),
-            jax.ShapeDtypeStruct((IMG, width), BF16),
-        ),
+        out_shape=shapes,
         in_specs=[anywhere] * 4 + [vmem] + [anywhere] * 3 + [smem, smem],
         out_specs=(vmem, vmem),
         scratch_shapes=[
@@ -616,6 +628,15 @@
         ),
         name="pool_contrast",
     )(patches, owner, slot, text, probe, w_key, w_value, w_out, scale, bias)
+    return pl.pallas_call(
+        hand_over,
+        out_shape=shapes,
+        in_specs=[anywhere, anywhere],
+        out_specs=(anywhere, anywhere),
+        scratch_shapes=[dma((2,))],
+        compiler_params=pltpu.CompilerParams(vmem_limit_bytes=56 * 2**20),
+        name="hand_over",
+    )(*grads)
 
 
 def solution(mesh):

time: 63.2 us -> 85.7 us (1.36)
  Pallas kernels: 57.8 us -> 83.7 us
  local copies, waits for them, and re-layouts: 3.23 us -> 0 us
    pallas_call x1 -> x2, Pallas kernels: 57.8 us -> 83.7 us  [the longest x1 64.4 us: local(): pl.pallas_call(functools.partial(kernel, nb, ng), out_shape=shapes, in_sp...]
    unnamed x2 -> x0, local copies, waits for them, and re-layouts: 3.23 us -> none
where the time goes in v3:
time: 85.7 us; the launch traced here: 85.6 us
  Pallas kernels  83.7 us (98%)
  between operations  1.93 us (2%)
    pallas_call x1, Pallas kernels, local(): pl.pallas_call(functools.partial(kernel, nb, ng), out_shape=shapes, in_sp...  64.4 us
    pallas_call x1, Pallas kernels, local(): pl.pallas_call(hand_over, out_shape=shapes, in_specs=[anywhere, anywhere]...  19.3 us

profile of v3, /device:TPU:1, one launch (start us, length us, event | category | flops | bytes accessed | tf_op | source)
XLA Modules:
  0.0 85.6 jit_solution(7645628723725253236)
XLA Ops:
  1.9 64.4 %pool_contrast.1 = (bf16[256,1152]{1,0:T(8,128)(2,1)}, bf16[4,1152]{1,0:T(4,128)(2,1)}) custom-call(bf16[256,1152]{1,0:T(8,128)(2,1)} %patches.1, s32[1,32,256]{2,1,0:T(8,128)} %owner_in.1, s32[1,32,256]{2,1,0:T(8,128)} %slot_in.1, bf16[4,1152]{1,0:T(4,128)(2,1)} %text_in.1, f32[1152]{0:T(1024)} %probe.1, bf16[1152,1152]{1,0:T(8,128)(2,1)} %w_key.1, ...), custom_call_target="tpu_custom_call" | custom-call | tf_op jit(solution)/shard_map/pool_contrast/pallas_call | solution.py:571
  66.3 19.3 %hand_over.1 = (bf16[256,1152]{1,0:T(8,128)(2,1)}, bf16[4,1152]{1,0:T(4,128)(2,1)}) custom-call(bf16[256,1152]{1,0:T(8,128)(2,1)} %get-tuple-element.4.patch_in, bf16[4,1152]{1,0:T(4,128)(2,1)} %get-tuple-element.5.text_in), custom_call_target="tpu_custom_call" | custom-call | tf_op jit(solution)/shard_map/hand_over/pallas_call | solution.py:631

commit v4 on v3

--- a/solution.py
+++ b/solution.py
@@ -54,8 +54,8 @@
     return y[0:IMG] + y[IMG : 2 * IMG] + y[2 * IMG : 3 * IMG]
 
 
-def far(j, n):
-    return (n // 2 + ((j + 1) // 2) * (2 * ((j + 1) % 2) - 1)) % n
+def far(n):
+    return [(n // 2 + ((j + 1) // 2) * (2 * ((j + 1) % 2) - 1)) % n for j in range(n)]
 
 
 def kernel(
@@ -94,44 +94,24 @@
     fs,
     rows16,
     pooled_buf,
-    unit_line,
+    unit_plane,
     u16,
     di_out,
     di_in,
-    unit_all,
     u64,
     t_img,
     tf,
-    t_txt,
     tt,
     td_out,
+    td_mid,
     td_in,
     pg_all,
     pgm,
     vg,
+    out,
     load_sem,
-    pair_send,
-    pair_recv,
-    tz_send,
-    tz_recv,
-    tx_send,
-    tx_recv,
-    tp_send,
-    tp_recv,
-    acc_send,
-    acc_recv,
-    uy_send,
-    uy_recv,
-    uz_send,
-    uz_recv,
-    di_send,
-    di_recv,
-    td_send,
-    td_recv,
-    pg_send,
-    pg_recv,
-    fw_send,
-    fw_recv,
+    send_sem,
+    recv_sem,
 ):
     nq = ng // 2
     nz = nq // X_HIGH
@@ -144,99 +124,59 @@
     head_width = width // HEADS
     blk = lax.axis_index("blk")
     grp = lax.axis_index("group")
-    core = grp % 2
-    q = grp // 2
-    z = q % nz
-    xh = q // nz
-    y = blk // X_LOW
-    x = xh * X_LOW + blk % X_LOW
+    core = lax.rem(grp, 2)
+    q = lax.div(grp, 2)
+    z = lax.rem(q, nz)
+    xh = lax.div(q, nz)
+    y = lax.div(blk, X_LOW)
+    x = xh * X_LOW + lax.rem(blk, X_LOW)
     xy = y * nx + x
     pending = []
 
     def at(x_, y_, z_, c_):
-        return (y_ * X_LOW + x_ % X_LOW, ((x_ // X_LOW) * nz + z_) * 2 + c_)
+        x_high = lax.div(x_, X_LOW)
+        return (y_ * X_LOW + x_ - x_high * X_LOW, (x_high * nz + z_) * 2 + c_)
+
+    def ring(pos, n):
+        return [pos if d == 0 else lax.rem(pos + d, n) for d in far(n)]
 
     sibling = at(x, y, z, 1 - core)
-
-    def group_peer(i):
-        k = ((xh + far(i // nz, X_HIGH)) % X_HIGH) * nz + (z + far(i % nz, nz)) % nz
-        return k, (blk, k * 2 + core)
-
-    def z_peer(i):
-        k = (z + far(i, nz)) % nz
-        return k, at(x, y, k, core)
-
-    def x_peer(i):
-        k = (x + far(i, nx)) % nx
-        return k, at(k, y, z, core)
-
-    def y_peer(i):
-        k = (y + far(i, ny)) % ny
-        return k, at(x, k, z, core)
-
-    def plane_peer(i):
-        y_ = (y + far(i // nx, ny)) % ny
-        x_ = (x + far(i % nx, nx)) % nx
-        return y_ * nx + x_, at(x_, y_, z, core)
-
-    def remote(src, dst, send, recv, device):
+    ring_x, ring_y, ring_z = ring(x, nx), ring(y, ny), ring(z, nz)
+    z_peers = [(k, at(x, y, k, core)) for k in ring_z[:-1]]
+    x_peers = [(k, at(k, y, z, core)) for k in ring_x[:-1]]
+    y_peers = [(k, at(x, k, z, core)) for k in ring_y[:-1]]
+    rest_peers = [(j * nx + k, at(k, j, z, core)) for k in ring_x[:-1] for j in ring_y]
+    far_peers = [
+        (h * nz + k, (blk, (h * nz + k) * 2 + core)) for h in ring(xh, X_HIGH)[:-1] for k in ring_z
+    ]
+    near_peers = [(xh * nz + k, device) for k, device in z_peers]
+
+    def remote(src, dst, n, device):
         return pltpu.make_async_remote_copy(
             src_ref=src,
             dst_ref=dst,
-            send_sem=send,
-            recv_sem=recv,
+            send_sem=send_sem.at[n],
+            recv_sem=recv_sem.at[n],
             device_id=device,
             device_id_type=MESH,
         )
 
-    def each(count, act):
-        def step(i, carry):
-            act(i)
-            return carry
-
-        lax.fori_loop(0, count - 1, step, 0)
-
-    def spread(peer, count, src_of, dst_of, me, send, recv):
-        def act(i):
-            k, device = peer(i)
-            remote(src_of(k), dst_of(me), send.at[k], recv.at[me], device).start()
-
-        each(count, act)
-
-        def settle(i):
-            k, device = peer(i)
-            remote(src_of(k), src_of(k), send.at[k], recv.at[k], device).wait_send()
-
-        pending.append(lambda: each(count, settle))
-
-    def gather_wait(peer, count, dst_of, send, recv, then=None):
-        def act(i):
-            k, device = peer(count - 2 - i)
-            remote(dst_of(k), dst_of(k), send.at[k], recv.at[k], device).wait_recv()
-            if then is not None:
-                then(k)
-
-        each(count, act)
+    def spread(peers, src_of, dst, n, whole):
+        for k, device in peers:
+            remote(src_of(k), dst, n, device).start()
+        pending.append((whole, n))
+
+    def arrived(whole, n):
+        remote(whole, whole, n, sibling).wait_recv()
 
     def to_sibling(src, dst, n):
-        copy = remote(src, dst, pair_send.at[n], pair_recv.at[n], sibling)
-        copy.start()
-        pending.append(copy.wait_send)
-
-    def from_sibling(dst, n):
-        remote(dst, dst, pair_send.at[n], pair_recv.at[n], sibling).wait_recv()
+        spread([(0, sibling)], lambda k: src, dst, n, src)
 
     barrier = pltpu.get_barrier_semaphore()
 
-    def greet(peer):
-        def act(i):
-            pl.semaphore_signal(barrier, inc=1, device_id=peer(i)[1], device_id_type=MESH)
-
-        return act
-
-    each(nq, greet(group_peer))
-    each(nxy, greet(plane_peer))
-    pl.semaphore_signal(barrier, inc=1, device_id=sibling, device_id_type=MESH)
+    greeted = far_peers + near_peers + rest_peers + y_peers + [(0, sibling)]
+    for _, device in greeted:
+        pl.semaphore_signal(barrier, inc=1, device_id=device, device_id_type=MESH)
 
     loads = [
         pltpu.make_async_copy(src, dst, load_sem.at[n])
@@ -320,12 +260,14 @@
     lax.fori_loop(0, chunks, pool, 0)
     loads[5].wait()
     t_img[(core * nx + x) * nz + z] = text[...]
-    t_txt[xy] = text[...]
-
-    pl.semaphore_wait(barrier, nq - 1 + nxy - 1 + 1)
+
+    pl.semaphore_wait(barrier, len(greeted))
     to_sibling(part_own.at[1 - core], part_in, 0)
-
-    from_sibling(part_in, 0)
+    t_here = (core * nx + x) * nz
+    slabs = lambda ref, n: ref.at[pl.ds(0, n)]
+    spread(z_peers, lambda k: text, t_img.at[t_here + z], 1, slabs(t_img, nz - 1))
+
+    arrived(part_in, 0)
     lane_m = lax.broadcasted_iota(jnp.int32, (mine, LANES), 1)
     stat_a = part_own[core, :, width : width + LANES]
     stat_b = part_in[:, width : width + LANES]
@@ -347,27 +289,18 @@
         )
         for k in range(nq):
             acc_out[k, :, cols] = total[k * IMG : (k + 1) * IMG]
-    acc_slab = lambda k: acc_in.at[k]
-    spread(group_peer, nq, lambda k: acc_out.at[k], acc_slab, q, acc_send, acc_recv)
-    z_slab = lambda k: t_img.at[(core * nx + x) * nz + k]
-    spread(z_peer, nz, lambda k: text, z_slab, z, tz_send, tz_recv)
-    spread(plane_peer, nxy, lambda k: text, lambda k: t_txt.at[k], xy, tp_send, tp_recv)
+    spread(far_peers + near_peers, lambda k: acc_out.at[k], acc_in.at[q], 2, slabs(acc_in, nq - 1))
     acc_in[q] = acc_out[q]
-    gather_wait(z_peer, nz, z_slab, tz_send, tz_recv)
-    x_slabs = lambda k: t_img.at[pl.ds((core * nx + k) * nz, nz)]
-    spread(x_peer, nx, lambda k: x_slabs(x), x_slabs, x, tx_send, tx_recv)
-    gather_wait(plane_peer, nxy, lambda k: t_txt.at[k], tp_send, tp_recv)
-    for k in range(nxy):
-        tt[k * IMG : (k + 1) * IMG, :] = t_txt[k].astype(F32)
-    tt_b = tt[...].astype(BF16)
-    tt_inv = 1.0 / jnp.sqrt(jnp.sum(tt[...] * tt[...], axis=1, keepdims=True) + EPS)
-    tt_inv = jnp.transpose(jnp.broadcast_to(tt_inv, (LANES, LANES)))[0:1, :]
-    gather_wait(x_peer, nx, x_slabs, tx_send, tx_recv)
+
+    arrived(slabs(t_img, nz - 1), 1)
+    x_part = t_img.at[pl.ds(t_here, nz)]
+    spread(x_peers, lambda k: x_part, x_part, 3, slabs(t_img, (nx - 1) * nz))
+    arrived(slabs(t_img, (nx - 1) * nz), 3)
     t_half = lambda c: t_img.at[pl.ds(c * nx * nz, nx * nz)]
-    to_sibling(t_half(core), t_half(core), 1)
+    to_sibling(t_half(core), t_half(core), 4)
     loads[6].wait()
 
-    gather_wait(group_peer, nq, acc_slab, acc_send, acc_recv)
+    arrived(slabs(acc_in, nq - 1), 2)
     lane4 = lax.broadcasted_iota(jnp.int32, (IMG, LANES), 1)
     heads4 = lane4 < HEADS
     parts = [acc_in[k, :, width : width + LANES] for k in range(nq)]
@@ -394,14 +327,11 @@
     embeds = three(mm(small_rows(pooled, rows16), wo[...]))
     norm = jnp.sqrt(jnp.sum(embeds * embeds, axis=1, keepdims=True) + EPS)
     unit = embeds / norm
-    unit_line[y] = unit
-    unit_all[core, z] = unit
-    y_slab = lambda k: unit_line.at[k]
-    spread(y_peer, ny, lambda k: unit_line.at[y], y_slab, y, uy_send, uy_recv)
-    u_slab = lambda k: unit_all.at[core, k]
-    spread(z_peer, nz, lambda k: unit_all.at[core, z], u_slab, z, uz_send, uz_recv)
-
-    from_sibling(t_half(1 - core), 1)
+    unit_plane[xy] = unit
+    u_here = unit_plane.at[xy]
+    spread(y_peers, lambda k: u_here, u_here, 5, slabs(unit_plane, ny - 1))
+
+    arrived(t_half(1 - core), 4)
     ntext = 2 * nx * nz * IMG
     for k in range(2 * nx * nz):
         tf[k * IMG : (k + 1) * IMG, :] = t_img[k].astype(F32)
@@ -409,37 +339,38 @@
     tb = texts.astype(BF16)
     inv = 1.0 / jnp.sqrt(jnp.sum(texts * texts, axis=1, keepdims=True) + EPS)
     inv_row = jnp.transpose(jnp.broadcast_to(inv, (ntext, LANES)))[0:1, :]
-    temper = jnp.exp(jnp.full((1, 1), logit_scale[0], F32))
+    temper = jnp.exp(logit_scale[...].reshape(1, 1))
+    offset = logit_bias[...].reshape(1, 1)
 
     def block_signal(u_pieces, tb_, inv_, image_slab, text_slab):
         n, t = u_pieces[0].shape[0], tb_.shape[0]
         dots = mm_nt(jnp.concatenate(u_pieces, axis=0).astype(BF16), tb_)
         dots = dots[0:n] + dots[n : 2 * n] + dots[2 * n : 3 * n]
-        logits = temper * (dots * inv_) + logit_bias[0]
+        logits = temper * (dots * inv_) + offset
         row = lax.broadcasted_iota(jnp.int32, (n, t), 0)
         col = lax.broadcasted_iota(jnp.int32, (n, t), 1)
         positive = ((row >> 2) == image_slab) & (col - text_slab * IMG == (row & (IMG - 1)))
         return 1.0 / (1.0 + jnp.exp(-logits)) - jnp.where(positive, 1.0, 0.0)
 
-    gather_wait(y_peer, ny, y_slab, uy_send, uy_recv)
+    arrived(slabs(unit_plane, ny - 1), 5)
     nline = ny * IMG
     for k in range(ny):
-        u16[k * IMG : (k + 1) * IMG, :] = unit_line[k]
+        u16[k * IMG : (k + 1) * IMG, :] = unit_plane[k * nx + x]
     signal = block_signal(pieces(u16[...], 3), tb, inv_row, y, (core * nx + x) * nz + z)
     di = mm(stacked(signal * inv_row, 3), tb)
     di = di[0:nline] + di[nline : 2 * nline] + di[2 * nline : 3 * nline]
     for k in range(ny):
         di_out[k] = di[k * IMG : (k + 1) * IMG]
-    di_slab = lambda k: di_in.at[k]
-    spread(y_peer, ny, lambda k: di_out.at[k], di_slab, y, di_send, di_recv)
+    spread(y_peers, lambda k: di_out.at[k], di_in.at[y], 6, slabs(di_in, ny - 1))
+    spread(rest_peers, lambda k: u_here, u_here, 7, slabs(unit_plane, (nx - 1) * ny))
     di_in[y] = di_out[y]
 
-    gather_wait(y_peer, ny, di_slab, di_send, di_recv)
+    arrived(slabs(di_in, ny - 1), 6)
     dunit = di_in[0]
     for k in range(1, ny):
         dunit = dunit + di_in[k]
     dunit = dunit * (temper * LOSS_SCALE)
-    unit = unit_line[y]
+    unit = unit_plane[xy]
     embed_grad = (dunit - unit * jnp.sum(unit * dunit, axis=1, keepdims=True)) / norm
     pooled_grad = three(mm_nt(small_rows(embed_grad, rows16), wo[...]))
     mass = three(mm_nt(small_rows(pooled_grad * pooled_buf[...], rows16), hm[...]))
@@ -447,45 +378,56 @@
     pg_all[core, q, :, width : width + LANES] = jnp.where(
         heads4, lse, jnp.where(lane4 < 2 * HEADS, mass, 0.0)
     )
-    pg_slab = lambda k: pg_all.at[core, k]
-    spread(group_peer, nq, lambda k: pg_slab(q), pg_slab, q, pg_send, pg_recv)
-
-    def forward(k):
-        remote(pg_slab(k), pg_slab(k), fw_send.at[k], fw_recv.at[k], sibling).start()
-
-    forward(q)
-
-    gather_wait(z_peer, nz, u_slab, uz_send, uz_recv)
-    to_sibling(unit_all.at[core], unit_all.at[core], 2)
-    from_sibling(unit_all.at[1 - core], 2)
+    pg_here = pg_all.at[core, q]
+    near = pg_all.at[core, pl.ds(xh * nz, nz)]
+    spread(far_peers, lambda k: pg_here, pg_here, 9, pg_all.at[0, pl.ds(0, nq - nz)])
+    spread(near_peers, lambda k: pg_here, pg_here, 10, pg_all.at[0, pl.ds(0, nz - 1)])
+
+    arrived(slabs(unit_plane, (nx - 1) * ny), 7)
+    for k in range(nxy):
+        u64[k * IMG : (k + 1) * IMG, :] = unit_plane[k]
     for c in range(2):
-        for k in range(nz):
-            r = (c * nz + k) * IMG
-            u64[r : r + IMG, :] = unit_all[c, k]
+        here = pl.ds(pl.multiple_of((c * nx + x) * nz * IMG, nz * IMG), nz * IMG)
+        tt[c * nz * IMG : (c + 1) * nz * IMG, :] = tf[here, :]
+    line_texts = tt[...]
+    line_inv = 1.0 / jnp.sqrt(jnp.sum(line_texts * line_texts, axis=1, keepdims=True) + EPS)
+    line_inv = jnp.transpose(jnp.broadcast_to(line_inv, (LANES, LANES)))[0:1, :]
     u_pieces = pieces(u64[...], 3)
-    s_hi, s_lo = pieces(block_signal(u_pieces, tt_b, tt_inv, core * nz + z, xy), 2)
-    gap = -6 * nz * IMG % LANES
+    signal = block_signal(u_pieces, line_texts.astype(BF16), line_inv, xy, core * nz + z)
+    s_hi, s_lo = pieces(signal, 2)
+    gap = -3 * nxy * IMG % LANES
     s_pad = jnp.concatenate([s_hi, s_hi, s_lo, jnp.zeros((gap, LANES), F32)], axis=0)
     u_pad = jnp.concatenate(
         [u_pieces[0], u_pieces[1], u_pieces[0], jnp.zeros((gap, width), F32)], axis=0
     )
     td = mm(jnp.transpose(s_pad).astype(BF16), u_pad.astype(BF16))
-    for k in range(nxy):
-        td_out[k] = td[k * IMG : (k + 1) * IMG]
-    td_slab = lambda k: td_in.at[k]
-    spread(plane_peer, nxy, lambda k: td_out.at[k], td_slab, xy, td_send, td_recv)
-    td_in[xy] = td_out[xy]
-
-    gather_wait(group_peer, nq, pg_slab, pg_send, pg_recv, forward)
+    for c in range(2):
+        for k in range(nz):
+            r = (c * nz + k) * IMG
+            td_out[c, k] = td[r : r + IMG]
+    to_sibling(td_out.at[1 - core], td_mid, 8)
+
+    arrived(pg_all.at[0, pl.ds(0, nz - 1)], 10)
+    to_sibling(near, near, 11)
+    arrived(td_mid, 8)
+    for k in range(nz):
+        td_out[core, k] = td_out[core, k] + td_mid[k]
+    spread(z_peers, lambda k: td_out.at[core, k], td_in.at[z], 12, slabs(td_in, nz - 1))
+    td_in[z] = td_out[core, z]
+    arrived(pg_all.at[0, pl.ds(0, nq - nz)], 9)
+    for k in range(X_HIGH - 1):
+        part = pg_all.at[core, pl.ds(lax.rem(xh + 1 + k, X_HIGH) * nz, nz)]
+        to_sibling(part, part, 13 + k)
     for k in range(nq):
         pgm[core, k * IMG : (k + 1) * IMG, :] = pg_all[core, k]
-
-    def arrived(k, carry):
-        other = pg_all.at[1 - core, k]
-        remote(other, other, fw_send.at[k], fw_recv.at[k], sibling).wait_recv()
-        return carry
-
-    lax.fori_loop(0, nq, arrived, 0)
+    arrived(near, 11)
+    for k in range(X_HIGH - 1):
+        arrived(near, 13 + k)
+
+    def store(j):
+        cols = slice(j * CHUNK, (j + 1) * CHUNK)
+        return pltpu.make_async_copy(out.at[:, cols], g_patch.at[:, cols], load_sem.at[7 + j])
+
     for k in range(nq):
         pgm[1 - core, k * IMG : (k + 1) * IMG, :] = pg_all[1 - core, k]
     row_stats = jnp.concatenate([pgm[0, :, width:], pgm[1, :, width:]], axis=0)
@@ -508,17 +450,16 @@
     vg[...] = stacked(mm(wt, hm[...]) * pgr, 2)
     et[...] = wt
 
-    def back(j, carry):
-        cols = pl.ds(pl.multiple_of(j * CHUNK, CHUNK), CHUNK)
+    for j in range(chunks):
+        cols = slice(j * CHUNK, (j + 1) * CHUNK)
         g = mm_nt(vg[...], wv[cols, :])
-        g_patch[:, cols] = (g[0:rows] + g[rows : 2 * rows] + mm(et[...], kpr[:, cols])).astype(BF16)
-        return carry
-
-    lax.fori_loop(0, chunks, back, 0)
-
-    gather_wait(plane_peer, nxy, td_slab, td_send, td_recv)
+        g = g[0:rows] + g[rows : 2 * rows] + mm(et[...], kpr[:, cols])
+        out[:, cols] = g.astype(BF16)
+        store(j).start()
+
+    arrived(slabs(td_in, nz - 1), 12)
     text_dunit = td_in[0]
-    for k in range(1, nxy):
+    for k in range(1, nz):
         text_dunit = text_dunit + td_in[k]
     text_dunit = text_dunit * (temper * LOSS_SCALE)
     own_text = text[...].astype(F32)
@@ -529,23 +470,28 @@
         / text_norm
     ).astype(BF16)
 
-    def forwarded(k, carry):
-        remote(pg_slab(k), pg_slab(k), fw_send.at[k], fw_recv.at[k], sibling).wait_send()
-        return carry
-
-    lax.fori_loop(0, nq, forwarded, 0)
-    for settle in pending:
-        settle()
-
-
-def hand_over(patch_in, text_in, patch_out, text_out, sem):
-    copies = [
-        pltpu.make_async_copy(patch_in, patch_out, sem.at[0]),
-        pltpu.make_async_copy(text_in, text_out, sem.at[1]),
+    for whole, n in pending:
+        remote(whole, whole, n, sibling).wait_send()
+    for j in range(chunks):
+        store(j).wait()
+
+
+def hand_over(patch_in, text_in, patch_out, text_out, patch, text, sem):
+    rows = patch.shape[0] // 2
+    halves = [slice(0, rows), slice(rows, 2 * rows)]
+    here = [
+        (patch_in.at[halves[0]], patch.at[halves[0]], patch_out.at[halves[0]]),
+        (patch_in.at[halves[1]], patch.at[halves[1]], patch_out.at[halves[1]]),
+        (text_in, text, text_out),
     ]
-    for copy in copies:
+    first = [pltpu.make_async_copy(a, b, sem.at[k]) for k, (a, b, _) in enumerate(here)]
+    then = [pltpu.make_async_copy(b, c, sem.at[3 + k]) for k, (_, b, c) in enumerate(here)]
+    for copy in first:
         copy.start()
-    for copy in copies:
+    for arrived, copy in zip(first, then):
+        arrived.wait()
+        copy.start()
+    for copy in then:
         copy.wait()
 
 
@@ -560,10 +506,8 @@
     wide = width + LANES
     vmem = pl.BlockSpec(memory_space=pltpu.VMEM)
     anywhere = pl.BlockSpec(memory_space=pl.ANY)
-    smem = pl.BlockSpec(memory_space=pltpu.SMEM)
     weight = pltpu.VMEM((width, width), BF16)
     dma = pltpu.SemaphoreType.DMA
-    two = lambda n: [dma((n,)), dma((n,))]
     shapes = (
         jax.ShapeDtypeStruct((rows, width), BF16),
         jax.ShapeDtypeStruct((IMG, width), BF16),
@@ -571,8 +515,8 @@
     grads = pl.pallas_call(
         functools.partial(kernel, nb, ng),
         out_shape=shapes,
-        in_specs=[anywhere] * 4 + [vmem] + [anywhere] * 3 + [smem, smem],
-        out_specs=(vmem, vmem),
+        in_specs=[anywhere] * 4 + [vmem] + [anywhere] * 3 + [vmem, vmem],
+        out_specs=(anywhere, vmem),
         scratch_shapes=[
             pltpu.VMEM(owner.shape, jnp.int32),
             pltpu.VMEM(slot.shape, jnp.int32),
@@ -595,33 +539,24 @@
             pltpu.VMEM((mine, LANES), F32),
             pltpu.VMEM((16, width), F32),
             pltpu.VMEM((IMG, width), F32),
-            pltpu.VMEM((ny, IMG, width), F32),
+            pltpu.VMEM((nxy, IMG, width), F32),
             pltpu.VMEM((ny * IMG, width), F32),
             pltpu.VMEM((ny, IMG, width), F32),
             pltpu.VMEM((ny, IMG, width), F32),
-            pltpu.VMEM((2, nz, IMG, width), F32),
-            pltpu.VMEM((2 * nz * IMG, width), F32),
+            pltpu.VMEM((nxy * IMG, width), F32),
             pltpu.VMEM((2 * nx * nz, IMG, width), BF16),
             pltpu.VMEM((2 * nx * nz * IMG, width), F32),
-            pltpu.VMEM((nxy, IMG, width), BF16),
             pltpu.VMEM((LANES, width), F32),
-            pltpu.VMEM((nxy, IMG, width), F32),
-            pltpu.VMEM((nxy, IMG, width), F32),
+            pltpu.VMEM((2, nz, IMG, width), F32),
+            pltpu.VMEM((nz, IMG, width), F32),
+            pltpu.VMEM((nz, IMG, width), F32),
             pltpu.VMEM((2, nq, IMG, wide), F32),
             pltpu.VMEM((2, mine, wide), F32),
             pltpu.VMEM((2 * rows, width), BF16),
-            dma((7,)),
-            *two(3),
-            *two(nz),
-            *two(nx),
-            *two(nxy),
-            *two(nq),
-            *two(ny),
-            *two(nz),
-            *two(ny),
-            *two(nxy),
-            *two(nq),
-            *two(nq),
+            pltpu.VMEM((rows, width), BF16),
+            dma((10,)),
+            dma((16,)),
+            dma((16,)),
         ],
         compiler_params=pltpu.CompilerParams(
             collective_id=0, has_side_effects=True, vmem_limit_bytes=56 * 2**20
@@ -633,7 +568,11 @@
         out_shape=shapes,
         in_specs=[anywhere, anywhere],
         out_specs=(anywhere, anywhere),
-        scratch_shapes=[dma((2,))],
+        scratch_shapes=[
+            pltpu.VMEM((rows, width), BF16),
+            pltpu.VMEM(text.shape, BF16),
+            dma((6,)),
+        ],
         compiler_params=pltpu.CompilerParams(vmem_limit_bytes=56 * 2**20),
         name="hand_over",
     )(*grads)

time: 85.7 us -> 55 us (0.64)
  Pallas kernels: 83.7 us -> 52.9 us
    pallas_call x1, Pallas kernels: 19.3 us -> 1.83 us  [local(): pl.pallas_call(hand_over, out_shape=shapes, in_specs=[anywhere, anywhere]...]
    pallas_call x1, Pallas kernels: 64.4 us -> 51.1 us  [local(): pl.pallas_call(functools.partial(kernel, nb, ng), out_shape=shapes, in_sp...]
where the time goes in v4:
time: 55 us; the launch traced here: 54.9 us
  Pallas kernels  52.9 us (96%)
  between operations  1.93 us (4%)
    pallas_call x1, Pallas kernels, local(): pl.pallas_call(functools.partial(kernel, nb, ng), out_shape=shapes, in_sp...  51.1 us
    pallas_call x1, Pallas kernels, local(): pl.pallas_call(hand_over, out_shape=shapes, in_specs=[anywhere, anywhere]...  1.83 us

profile of v4, /device:TPU:1, one launch (start us, length us, event | category | flops | bytes accessed | tf_op | source)
XLA Modules:
  0.0 54.9 jit_solution(12232139006700464375)
XLA Ops:
  1.9 51.1 %pool_contrast.1 = (bf16[256,1152]{1,0:T(8,128)(2,1)}, bf16[4,1152]{1,0:T(4,128)(2,1)}) custom-call(bf16[256,1152]{1,0:T(8,128)(2,1)} %patches.1, s32[1,32,256]{2,1,0:T(8,128)} %owner_in.1, s32[1,32,256]{2,1,0:T(8,128)} %slot_in.1, bf16[4,1152]{1,0:T(4,128)(2,1)} %text_in.1, f32[1152]{0:T(1024)} %probe.1, bf16[1152,1152]{1,0:T(8,128)(2,1)} %w_key.1, ...), custom_call_target="tpu_custom_call" | custom-call | tf_op jit(solution)/shard_map/pool_contrast/pallas_call | solution.py:515
  53.0 1.8 %hand_over.1 = (bf16[256,1152]{1,0:T(8,128)(2,1)}, bf16[4,1152]{1,0:T(4,128)(2,1)}) custom-call(bf16[256,1152]{1,0:T(8,128)(2,1)} %get-tuple-element.4.patch_in, bf16[4,1152]{1,0:T(4,128)(2,1)} %get-tuple-element.5.text_in), custom_call_target="tpu_custom_call" | custom-call | tf_op jit(solution)/shard_map/hand_over/pallas_call | solution.py:566

commit v5 on v4

--- a/solution.py
+++ b/solution.py
@@ -13,6 +13,7 @@
 X_LOW, X_HIGH = 2, 2
 LANES = 128
 CHUNK = 384
+SPLIT = 512
 LOSS_SCALE = 256.0
 EPS = 1e-06
 LOW = -1e30
@@ -65,7 +66,7 @@
     owner_in,
     slot_in,
     text_in,
-    probe,
+    probe_in,
     w_key,
     w_value,
     w_out,
@@ -76,6 +77,7 @@
     owner,
     slot,
     text,
+    probe,
     wk,
     wv,
     wo,
@@ -87,6 +89,7 @@
     kpr,
     ot,
     et,
+    ob,
     part_own,
     part_in,
     acc_out,
@@ -172,59 +175,66 @@
     def to_sibling(src, dst, n):
         spread([(0, sibling)], lambda k: src, dst, n, src)
 
+    pieces_of = [slice(j * CHUNK, (j + 1) * CHUNK) for j in range(chunks)]
+    halves = [slice(0, SPLIT), slice(SPLIT, width)]
+
+    def load(n, src, dst):
+        copy = pltpu.make_async_copy(src, dst, load_sem.at[n])
+        copy.start()
+        return copy
+
+    load_probe = load(chunks, probe_in, probe)
+    load_rows = [
+        load(chunks + 1, owner_in, owner),
+        load(chunks + 2, slot_in, slot),
+    ]
+    load_k = [load(j, w_key.at[cols], wk.at[cols]) for j, cols in enumerate(pieces_of)]
+    load_rows.append(load(chunks + 3, patches, p))
+    load_text = [
+        load(chunks + 4, text_in, text),
+    ]
+    late = chunks + 7
+    load_v = [load(late + j, w_value.at[cols], wv.at[cols]) for j, cols in enumerate(pieces_of)]
+    load_o = load(late + chunks, w_out, wo)
+
     barrier = pltpu.get_barrier_semaphore()
 
     greeted = far_peers + near_peers + rest_peers + y_peers + [(0, sibling)]
     for _, device in greeted:
         pl.semaphore_signal(barrier, inc=1, device_id=device, device_id_type=MESH)
-
-    loads = [
-        pltpu.make_async_copy(src, dst, load_sem.at[n])
-        for n, (src, dst) in enumerate(
-            [
-                (w_key, wk),
-                (owner_in, owner),
-                (slot_in, slot),
-                (patches, p),
-                (w_value, wv),
-                (text_in, text),
-                (w_out, wo),
-            ]
-        )
-    ]
-    for load in loads:
-        load.start()
 
     row_i = lax.broadcasted_iota(jnp.int32, (LANES, width), 0)
     col_i = lax.broadcasted_iota(jnp.int32, (LANES, width), 1)
     first = (row_i & (HEADS - 1)) * head_width
     in_head = (col_i >= first) & (col_i < first + head_width)
     hm[...] = jnp.where(in_head & (row_i < 3 * HEADS), 1.0, 0.0).astype(BF16)
+    load_probe.wait()
     q3 = pieces(probe[...].reshape(1, width) / math.sqrt(head_width), 3)
     band = lax.broadcasted_iota(jnp.int32, (3 * HEADS, width), 0) // HEADS
     q_rows = jnp.where(band == 0, q3[0], jnp.where(band == 1, q3[1], q3[2]))
     table = (q_rows * hm[0 : 3 * HEADS, :].astype(F32)).astype(BF16)
-    loads[0].wait()
-    kpt = mm_nt(table, wk[...])
-    kp = kpt[0:HEADS] + kpt[HEADS : 2 * HEADS] + kpt[2 * HEADS : 3 * HEADS]
-    kp_pieces = pieces(kp, 3)
-    kp3[...] = jnp.concatenate(kp_pieces, axis=0).astype(BF16)
     kpr[...] = jnp.zeros_like(kpr)
-    kpr[3 * HEADS : 6 * HEADS, :] = jnp.concatenate(
-        [kp_pieces[0], kp_pieces[1], kp_pieces[0]], axis=0
-    ).astype(BF16)
+    for j, cols in enumerate(pieces_of):
+        load_k[j].wait()
+        kpt = mm_nt(table, wk[cols, :])
+        kp = kpt[0:HEADS] + kpt[HEADS : 2 * HEADS] + kpt[2 * HEADS : 3 * HEADS]
+        kp_pieces = pieces(kp, 3)
+        kp3[:, cols] = jnp.concatenate(kp_pieces, axis=0).astype(BF16)
+        kpr[3 * HEADS : 6 * HEADS, cols] = jnp.concatenate(
+            [kp_pieces[0], kp_pieces[1], kp_pieces[0]], axis=0
+        ).astype(BF16)
     rows16[...] = jnp.zeros_like(rows16)
     tt[...] = jnp.zeros_like(tt)
 
-    loads[1].wait()
-    loads[2].wait()
+    load_rows[0].wait()
+    load_rows[1].wait()
     own_owner = owner[0, pl.ds(grp, 1), :]
     code = (own_owner & 1) * mine + (own_owner >> 1) * IMG + slot[0, pl.ds(grp, 1), :]
     member = code == lax.broadcasted_iota(jnp.int32, (2 * mine, rows), 0)
     ot_f = jnp.where(member, 1.0, 0.0)
     ot[...] = ot_f.astype(BF16)
 
-    loads[3].wait()
+    load_rows[2].wait()
     s = mm_nt(kp3[...], p[...])
     scores = s[0:HEADS] + s[HEADS : 2 * HEADS] + s[2 * HEADS : 3 * HEADS]
     st[...] = scores
@@ -245,29 +255,28 @@
     stats = jnp.where(lane < HEADS, peak, mm(ot[...], et[...]))
     for c in range(2):
         part_own[c, :, width : width + LANES] = stats[c * mine : (c + 1) * mine]
-    loads[4].wait()
-
-    def pool(j, carry):
-        cols = pl.ds(pl.multiple_of(j * CHUNK, CHUNK), CHUNK)
+    for copy in load_v:
+        copy.wait()
+    for cols in halves:
         value = mm(p[...], wv[:, cols])
         v[:, cols] = value
         x_hi, x_lo = pieces(mm(et[...], hm[:, cols]) * value, 2)
         total = mm(ot[...], x_hi.astype(BF16)) + mm(ot[...], x_lo.astype(BF16))
         for c in range(2):
             part_own[c, :, cols] = total[c * mine : (c + 1) * mine]
-        return carry
-
-    lax.fori_loop(0, chunks, pool, 0)
-    loads[5].wait()
+    for copy in load_text:
+        copy.wait()
     t_img[(core * nx + x) * nz + z] = text[...]
 
     pl.semaphore_wait(barrier, len(greeted))
-    to_sibling(part_own.at[1 - core], part_in, 0)
+    part_cols = [slice(width, width + LANES)] + halves
+    for j, cols in enumerate(part_cols):
+        to_sibling(part_own.at[1 - core, :, cols], part_in.at[:, cols], 16 + j)
     t_here = (core * nx + x) * nz
     slabs = lambda ref, n: ref.at[pl.ds(0, n)]
     spread(z_peers, lambda k: text, t_img.at[t_here + z], 1, slabs(t_img, nz - 1))
 
-    arrived(part_in, 0)
+    arrived(part_in.at[:, part_cols[0]], 16)
     lane_m = lax.broadcasted_iota(jnp.int32, (mine, LANES), 1)
     stat_a = part_own[core, :, width : width + LANES]
     stat_b = part_in[:, width : width + LANES]
@@ -281,8 +290,8 @@
         scale.append((f_hi + pltpu.roll(f_lo, HEADS, 1)).astype(BF16))
     for k in range(nq):
         acc_out[k, :, width : width + LANES] = chip_stats[k * IMG : (k + 1) * IMG]
-    for j in range(chunks):
-        cols = slice(j * CHUNK, (j + 1) * CHUNK)
+    for j, cols in enumerate(halves):
+        arrived(part_in.at[:, cols], 17 + j)
         total = (
             mm(scale[0], hm[:, cols]) * part_own[core, :, cols]
             + mm(scale[1], hm[:, cols]) * part_in[:, cols]
@@ -298,7 +307,11 @@
     arrived(slabs(t_img, (nx - 1) * nz), 3)
     t_half = lambda c: t_img.at[pl.ds(c * nx * nz, nx * nz)]
     to_sibling(t_half(core), t_half(core), 4)
-    loads[6].wait()
+    load_o.wait()
+
+    for c in range(2):
+        half = ot_f[c * mine : (c + 1) * mine]
+        ob[c] = jnp.transpose(jnp.concatenate([half, half], axis=0)).astype(BF16)
 
     arrived(slabs(acc_in, nq - 1), 2)
     lane4 = lax.broadcasted_iota(jnp.int32, (IMG, LANES), 1)
@@ -339,8 +352,8 @@
     tb = texts.astype(BF16)
     inv = 1.0 / jnp.sqrt(jnp.sum(texts * texts, axis=1, keepdims=True) + EPS)
     inv_row = jnp.transpose(jnp.broadcast_to(inv, (ntext, LANES)))[0:1, :]
-    temper = jnp.exp(logit_scale[...].reshape(1, 1))
-    offset = logit_bias[...].reshape(1, 1)
+    temper = jnp.exp(jnp.full((1, 1), logit_scale[0], F32))
+    offset = logit_bias[0]
 
     def block_signal(u_pieces, tb_, inv_, image_slab, text_slab):
         n, t = u_pieces[0].shape[0], tb_.shape[0]
@@ -420,13 +433,14 @@
         to_sibling(part, part, 13 + k)
     for k in range(nq):
         pgm[core, k * IMG : (k + 1) * IMG, :] = pg_all[core, k]
+    pgr = mm(ob[core], stacked(pgm[core, :, 0:width], 2))
     arrived(near, 11)
     for k in range(X_HIGH - 1):
         arrived(near, 13 + k)
 
     def store(j):
-        cols = slice(j * CHUNK, (j + 1) * CHUNK)
-        return pltpu.make_async_copy(out.at[:, cols], g_patch.at[:, cols], load_sem.at[7 + j])
+        cols = halves[j]
+        return pltpu.make_async_copy(out.at[:, cols], g_patch.at[:, cols], load_sem.at[j])
 
     for k in range(nq):
         pgm[1 - core, k * IMG : (k + 1) * IMG, :] = pg_all[1 - core, k]
@@ -435,25 +449,21 @@
     row_stats = (
         row_stats[0 : 2 * HEADS] + row_stats[2 * HEADS : 4 * HEADS] + row_stats[4 * HEADS : 6 * HEADS]
     )
-    own_o = jnp.transpose(jnp.concatenate([ot_f, ot_f], axis=0)).astype(BF16)
-    pg = jnp.concatenate([pgm[0, :, 0:width], pgm[1, :, 0:width]], axis=0)
-    pgr = mm(own_o, stacked(pg, 2))
+    pgr = pgr + mm(ob[1 - core], stacked(pgm[1 - core, :, 0:width], 2))
+    w = jnp.exp(st[...] - row_stats[0:HEADS])
+    gap = jnp.zeros((LANES - 2 * HEADS, rows), F32)
+    w_t = jnp.transpose(jnp.concatenate(pieces(w, 2) + [gap], axis=0)).astype(BF16)
+    vg[...] = stacked(mm(w_t, hm[...]) * pgr, 2)
     d_hi, d_lo = pieces(pgr * v[...], 2)
     dw = mm_nt(hm[0:HEADS, :], d_hi.astype(BF16)) + mm_nt(hm[0:HEADS, :], d_lo.astype(BF16))
-    w = jnp.exp(st[...] - row_stats[0:HEADS])
-    ds = w * (dw - row_stats[HEADS : 2 * HEADS])
-    w_hi, w_lo = pieces(w, 2)
-    ds_hi, ds_lo = pieces(ds, 2)
-    wt = jnp.transpose(
-        jnp.concatenate([w_hi, w_lo, blank, ds_hi, ds_hi, ds_lo, blank, blank], axis=0)
+    ds_hi, ds_lo = pieces(w * (dw - row_stats[HEADS : 2 * HEADS]), 2)
+    ds_t = jnp.transpose(
+        jnp.concatenate([blank, blank, blank, ds_hi, ds_hi, ds_lo, blank, blank], axis=0)
     ).astype(BF16)
-    vg[...] = stacked(mm(wt, hm[...]) * pgr, 2)
-    et[...] = wt
-
-    for j in range(chunks):
-        cols = slice(j * CHUNK, (j + 1) * CHUNK)
+
+    for j, cols in enumerate(halves):
         g = mm_nt(vg[...], wv[cols, :])
-        g = g[0:rows] + g[rows : 2 * rows] + mm(et[...], kpr[:, cols])
+        g = g[0:rows] + g[rows : 2 * rows] + mm(ds_t, kpr[:, cols])
         out[:, cols] = g.astype(BF16)
         store(j).start()
 
@@ -472,7 +482,7 @@
 
     for whole, n in pending:
         remote(whole, whole, n, sibling).wait_send()
-    for j in range(chunks):
+    for j in range(len(halves)):
         store(j).wait()
 
 
@@ -515,12 +525,13 @@
     grads = pl.pallas_call(
         functools.partial(kernel, nb, ng),
         out_shape=shapes,
-        in_specs=[anywhere] * 4 + [vmem] + [anywhere] * 3 + [vmem, vmem],
+        in_specs=[anywhere] * 8 + [pl.BlockSpec(memory_space=pltpu.SMEM)] * 2,
         out_specs=(anywhere, vmem),
         scratch_shapes=[
             pltpu.VMEM(owner.shape, jnp.int32),
             pltpu.VMEM(slot.shape, jnp.int32),
             pltpu.VMEM(text.shape, BF16),
+            pltpu.VMEM((width,), F32),
             weight,
             weight,
             weight,
@@ -532,6 +543,7 @@
             pltpu.VMEM((LANES, width), BF16),
             pltpu.VMEM((2 * mine, rows), BF16),
             pltpu.VMEM((rows, LANES), BF16),
+            pltpu.VMEM((2, rows, 2 * mine), BF16),
             pltpu.VMEM((2, mine, wide), F32),
             pltpu.VMEM((mine, wide), F32),
             pltpu.VMEM((nq, IMG, wide), F32),
@@ -554,9 +566,9 @@
             pltpu.VMEM((2, mine, wide), F32),
             pltpu.VMEM((2 * rows, width), BF16),
             pltpu.VMEM((rows, width), BF16),
-            dma((10,)),
             dma((16,)),
-            dma((16,)),
+            dma((20,)),
+            dma((20,)),
         ],
         compiler_params=pltpu.CompilerParams(
             collective_id=0, has_side_effects=True, vmem_limit_bytes=56 * 2**20

time: 55 us -> 52.2 us (0.949)
  Pallas kernels: 52.9 us -> 50.1 us
    pallas_call x1, Pallas kernels: 51.1 us -> 48.3 us  [local(): pl.pallas_call(functools.partial(kernel, nb, ng), out_shape=shapes, in_sp...]
where the time goes in v5:
time: 52.2 us; the launch traced here: 52.1 us
  Pallas kernels  50.1 us (96%)
  between operations  1.93 us (4%)
    pallas_call x1, Pallas kernels, local(): pl.pallas_call(functools.partial(kernel, nb, ng), out_shape=shapes, in_sp...  48.3 us
    pallas_call x1, Pallas kernels, local(): pl.pallas_call(hand_over, out_shape=shapes, in_specs=[anywhere, anywhere]...  1.83 us

profile of v5, /device:TPU:1, one launch (start us, length us, event | category | flops | bytes accessed | tf_op | source)
XLA Modules:
  0.0 52.1 jit_solution(4017912729637094723)
XLA Ops:
  1.9 48.3 %pool_contrast.1 = (bf16[256,1152]{1,0:T(8,128)(2,1)}, bf16[4,1152]{1,0:T(4,128)(2,1)}) custom-call(bf16[256,1152]{1,0:T(8,128)(2,1)} %patches.1, s32[1,32,256]{2,1,0:T(8,128)} %owner_in.1, s32[1,32,256]{2,1,0:T(8,128)} %slot_in.1, bf16[4,1152]{1,0:T(4,128)(2,1)} %text_in.1, f32[1152]{0:T(1024)} %probe_in.1, bf16[1152,1152]{1,0:T(8,128)(2,1)} %w_key.1, ...), custom_call_target="tpu_custom_call" | custom-call | tf_op jit(solution)/shard_map/pool_contrast/pallas_call | solution.py:525
  50.2 1.8 %hand_over.1 = (bf16[256,1152]{1,0:T(8,128)(2,1)}, bf16[4,1152]{1,0:T(4,128)(2,1)}) custom-call(bf16[256,1152]{1,0:T(8,128)(2,1)} %get-tuple-element.4.patch_in, bf16[4,1152]{1,0:T(4,128)(2,1)} %get-tuple-element.5.text_in), custom_call_target="tpu_custom_call" | custom-call | tf_op jit(solution)/shard_map/hand_over/pallas_call | solution.py:578

commit v6 on v5

--- a/solution.py
+++ b/solution.py
@@ -112,6 +112,7 @@
     pgm,
     vg,
     out,
+    text_out,
     load_sem,
     send_sem,
     recv_sem,
@@ -171,6 +172,10 @@
 
     def arrived(whole, n):
         remote(whole, whole, n, sibling).wait_recv()
+
+    def settle(sends):
+        for whole, n in sends:
+            remote(whole, whole, n, sibling).wait_send()
 
     def to_sibling(src, dst, n):
         spread([(0, sibling)], lambda k: src, dst, n, src)
@@ -391,6 +396,7 @@
     pg_all[core, q, :, width : width + LANES] = jnp.where(
         heads4, lse, jnp.where(lane4 < 2 * HEADS, mass, 0.0)
     )
+    early, pending = pending, []
     pg_here = pg_all.at[core, q]
     near = pg_all.at[core, pl.ds(xh * nz, nz)]
     spread(far_peers, lambda k: pg_here, pg_here, 9, pg_all.at[0, pl.ds(0, nq - nz)])
@@ -420,6 +426,8 @@
             td_out[c, k] = td[r : r + IMG]
     to_sibling(td_out.at[1 - core], td_mid, 8)
 
+    settle(early)
+
     arrived(pg_all.at[0, pl.ds(0, nz - 1)], 10)
     to_sibling(near, near, 11)
     arrived(td_mid, 8)
@@ -475,15 +483,17 @@
     own_text = text[...].astype(F32)
     text_norm = jnp.sqrt(jnp.sum(own_text * own_text, axis=1, keepdims=True) + EPS)
     text_unit = own_text / text_norm
-    g_text[...] = (
+    text_out[...] = (
         (text_dunit - text_unit * jnp.sum(text_unit * text_dunit, axis=1, keepdims=True))
         / text_norm
     ).astype(BF16)
 
-    for whole, n in pending:
-        remote(whole, whole, n, sibling).wait_send()
+    store_text = pltpu.make_async_copy(text_out, g_text, load_sem.at[len(halves)])
+    store_text.start()
+    settle(pending)
     for j in range(len(halves)):
         store(j).wait()
+    store_text.wait()
 
 
 def hand_over(patch_in, text_in, patch_out, text_out, patch, text, sem):
@@ -514,7 +524,6 @@
     nxy = nx * ny
     mine = nq * IMG
     wide = width + LANES
-    vmem = pl.BlockSpec(memory_space=pltpu.VMEM)
     anywhere = pl.BlockSpec(memory_space=pl.ANY)
     weight = pltpu.VMEM((width, width), BF16)
     dma = pltpu.SemaphoreType.DMA
@@ -526,7 +535,7 @@
         functools.partial(kernel, nb, ng),
         out_shape=shapes,
         in_specs=[anywhere] * 8 + [pl.BlockSpec(memory_space=pltpu.SMEM)] * 2,
-        out_specs=(anywhere, vmem),
+        out_specs=(anywhere, anywhere),
         scratch_shapes=[
             pltpu.VMEM(owner.shape, jnp.int32),
             pltpu.VMEM(slot.shape, jnp.int32),
@@ -566,6 +575,7 @@
             pltpu.VMEM((2, mine, wide), F32),
             pltpu.VMEM((2 * rows, width), BF16),
             pltpu.VMEM((rows, width), BF16),
+            pltpu.VMEM(text.shape, BF16),
             dma((16,)),
             dma((20,)),
             dma((20,)),

time: 52.2 us -> 51.7 us (level)
    pallas_call x1, Pallas kernels: 48.3 us -> 47.8 us  [local(): pl.pallas_call(functools.partial(kernel, nb, ng), out_shape=shapes, in_sp...]
where the time goes in v6:
time: 51.7 us; the launch traced here: 51.5 us
  Pallas kernels  49.6 us (96%)
  between operations  1.93 us (4%)
    pallas_call x1, Pallas kernels, local(): pl.pallas_call(functools.partial(kernel, nb, ng), out_shape=shapes, in_sp...  47.8 us
    pallas_call x1, Pallas kernels, local(): pl.pallas_call(hand_over, out_shape=shapes, in_specs=[anywhere, anywhere]...  1.83 us

profile of v6, /device:TPU:1, one launch (start us, length us, event | category | flops | bytes accessed | tf_op | source)
XLA Modules:
  0.0 51.5 jit_solution(14805127904459480642)
XLA Ops:
  1.9 47.8 %pool_contrast.1 = (bf16[256,1152]{1,0:T(8,128)(2,1)}, bf16[4,1152]{1,0:T(4,128)(2,1)}) custom-call(bf16[256,1152]{1,0:T(8,128)(2,1)} %patches.1, s32[1,32,256]{2,1,0:T(8,128)} %owner_in.1, s32[1,32,256]{2,1,0:T(8,128)} %slot_in.1, bf16[4,1152]{1,0:T(4,128)(2,1)} %text_in.1, f32[1152]{0:T(1024)} %probe_in.1, bf16[1152,1152]{1,0:T(8,128)(2,1)} %w_key.1, ...), custom_call_target="tpu_custom_call" | custom-call | tf_op jit(solution)/shard_map/pool_contrast/pallas_call | solution.py:534
  49.7 1.8 %hand_over.1 = (bf16[256,1152]{1,0:T(8,128)(2,1)}, bf16[4,1152]{1,0:T(4,128)(2,1)}) custom-call(bf16[256,1152]{1,0:T(8,128)(2,1)} %get-tuple-element.4.patch_in, bf16[4,1152]{1,0:T(4,128)(2,1)} %get-tuple-element.5.text_in), custom_call_target="tpu_custom_call" | custom-call | tf_op jit(solution)/shard_map/hand_over/pallas_call | solution.py:588

commit v7 on v6

--- a/solution.py
+++ b/solution.py
@@ -13,7 +13,7 @@
 X_LOW, X_HIGH = 2, 2
 LANES = 128
 CHUNK = 384
-SPLIT = 512
+SPLIT = 640
 LOSS_SCALE = 256.0
 EPS = 1e-06
 LOW = -1e30
@@ -497,15 +497,12 @@
 
 
 def hand_over(patch_in, text_in, patch_out, text_out, patch, text, sem):
-    rows = patch.shape[0] // 2
-    halves = [slice(0, rows), slice(rows, 2 * rows)]
-    here = [
-        (patch_in.at[halves[0]], patch.at[halves[0]], patch_out.at[halves[0]]),
-        (patch_in.at[halves[1]], patch.at[halves[1]], patch_out.at[halves[1]]),
-        (text_in, text, text_out),
-    ]
+    rows = patch.shape[0] // 4
+    parts = [slice(k * rows, (k + 1) * rows) for k in range(4)]
+    here = [(patch_in.at[part], patch.at[part], patch_out.at[part]) for part in parts]
+    here.append((text_in, text, text_out))
     first = [pltpu.make_async_copy(a, b, sem.at[k]) for k, (a, b, _) in enumerate(here)]
-    then = [pltpu.make_async_copy(b, c, sem.at[3 + k]) for k, (_, b, c) in enumerate(here)]
+    then = [pltpu.make_async_copy(b, c, sem.at[5 + k]) for k, (_, b, c) in enumerate(here)]
     for copy in first:
         copy.start()
     for arrived, copy in zip(first, then):
@@ -593,7 +590,7 @@
         scratch_shapes=[
             pltpu.VMEM((rows, width), BF16),
             pltpu.VMEM(text.shape, BF16),
-            dma((6,)),
+            dma((10,)),
         ],
         compiler_params=pltpu.CompilerParams(vmem_limit_bytes=56 * 2**20),
         name="hand_over",

time: 51.7 us -> 52.5 us (1.015)
  Pallas kernels: 49.6 us -> 50.4 us
    pallas_call x1, Pallas kernels: 47.8 us -> 48.6 us  [local(): pl.pallas_call(functools.partial(kernel, nb, ng), out_shape=shapes, in_sp...]
where the time goes in v7:
time: 52.5 us; the launch traced here: 52.4 us
  Pallas kernels  50.4 us (96%)
  between operations  1.93 us (4%)
    pallas_call x1, Pallas kernels, local(): pl.pallas_call(functools.partial(kernel, nb, ng), out_shape=shapes, in_sp...  48.6 us
    pallas_call x1, Pallas kernels, local(): pl.pallas_call(hand_over, out_shape=shapes, in_specs=[anywhere, anywhere]...  1.87 us

profile of v7, /device:TPU:1, one launch (start us, length us, event | category | flops | bytes accessed | tf_op | source)
XLA Modules:
  0.0 52.4 jit_solution(7833790349589131224)
XLA Ops:
  1.9 48.6 %pool_contrast.1 = (bf16[256,1152]{1,0:T(8,128)(2,1)}, bf16[4,1152]{1,0:T(4,128)(2,1)}) custom-call(bf16[256,1152]{1,0:T(8,128)(2,1)} %patches.1, s32[1,32,256]{2,1,0:T(8,128)} %owner_in.1, s32[1,32,256]{2,1,0:T(8,128)} %slot_in.1, bf16[4,1152]{1,0:T(4,128)(2,1)} %text_in.1, f32[1152]{0:T(1024)} %probe_in.1, bf16[1152,1152]{1,0:T(8,128)(2,1)} %w_key.1, ...), custom_call_target="tpu_custom_call" | custom-call | tf_op jit(solution)/shard_map/pool_contrast/pallas_call | solution.py:531
  50.5 1.9 %hand_over.1 = (bf16[256,1152]{1,0:T(8,128)(2,1)}, bf16[4,1152]{1,0:T(4,128)(2,1)}) custom-call(bf16[256,1152]{1,0:T(8,128)(2,1)} %get-tuple-element.4.patch_in, bf16[4,1152]{1,0:T(4,128)(2,1)} %get-tuple-element.5.text_in), custom_call_target="tpu_custom_call" | custom-call | tf_op jit(solution)/shard_map/hand_over/pallas_call | solution.py:585
